TPU v7x, 128 devices: a whole 4x4x4 slice. The times are simulated.
128 devices in a mesh: dp: 16 (over z, x_hi, core), sub: 8 (over x_lo, y).
Axes of the slice: x: 4 (x_hi: 2, x_lo: 2; x = x_hi * 2 + x_lo), y: 4, z: 4, core: 2. Of those that a mesh axis runs over, the one named last changes fastest.
Arguments:
- tokens: bfloat16 [16384, 768], P(('dp', 'sub')), may hold values from -6 to 6
- cotangent: bfloat16 [16384, 768], P(('dp', 'sub')), may hold values from -6 to 6
- seq_lengths: int32 [128, 4], P(('dp', 'sub')), may hold values from 0 to 128, as said below
- norm_gain: bfloat16 [768], P(('dp', 'sub')), may hold values from 0.5 to 1.5
- weight_query: bfloat16 [768, 768], P(('dp', 'sub')), may hold values from -0.21875 to 0.21875
- weight_key: bfloat16 [768, 768], P(('dp', 'sub')), may hold values from -0.21875 to 0.21875
- weight_value: bfloat16 [768, 768], P(('dp', 'sub')), may hold values from -0.21875 to 0.21875
- weight_rate: bfloat16 [768, 12], P(('dp', 'sub')), may hold values from -0.21875 to 0.21875
- bias_rate: bfloat16 [12], replicated, may hold values from -3 to 3
- init_weight: bfloat16 [768, 64], P(('dp', 'sub')), may hold values from -0.75 to 0.75
- init_bias: bfloat16 [768], P(('dp', 'sub')), may hold values from -3 to 3
- inner_gain: bfloat16 [768], P(('dp', 'sub')), may hold values from 0.5 to 1.5
- inner_bias: bfloat16 [768], P(('dp', 'sub')), may hold values from -3 to 3
- post_gain: bfloat16 [768], P(('dp', 'sub')), may hold values from 0.5 to 1.5
- post_bias: bfloat16 [768], P(('dp', 'sub')), may hold values from -3 to 3
- weight_out: bfloat16 [768, 768], P(('dp', 'sub')), may hold values from -0.21875 to 0.21875
- mlp_gain: bfloat16 [768], P(('dp', 'sub')), may hold values from 0.5 to 1.5
- weight_gate: bfloat16 [768, 2048], P(('dp', 'sub')), may hold values from -0.21875 to 0.21875
- weight_up: bfloat16 [768, 2048], P(('dp', 'sub')), may hold values from -0.21875 to 0.21875
- weight_down: bfloat16 [768, 2048], P(('dp', 'sub')), may hold values from -0.125 to 0.125
Outputs:
- output: bfloat16 [16384, 768], P(('dp', 'sub'))
- grad_tokens: bfloat16 [16384, 768], P(('dp', 'sub'))
- grad_norm_gain: float32 [768], P(('dp', 'sub'))
- grad_query: float32 [768, 768], P(('dp', 'sub'))
- grad_key: float32 [768, 768], P(('dp', 'sub'))
- grad_value: float32 [768, 768], P(('dp', 'sub'))
- grad_rate: float32 [768, 12], P(('dp', 'sub'))
- grad_bias_rate: float32 [12], replicated
- grad_init_weight: float32 [768, 64], P(('dp', 'sub'))
- grad_init_bias: float32 [768], P(('dp', 'sub'))
- grad_inner_gain: float32 [768], P(('dp', 'sub'))
- grad_inner_bias: float32 [768], P(('dp', 'sub'))
- grad_post_gain: float32 [768], P(('dp', 'sub'))
- grad_post_bias: float32 [768], P(('dp', 'sub'))
- grad_out: float32 [768, 768], P(('dp', 'sub'))
- grad_mlp_gain: float32 [768], P(('dp', 'sub'))
- grad_gate: float32 [768, 2048], P(('dp', 'sub'))
- grad_up: float32 [768, 2048], P(('dp', 'sub'))
- grad_down: float32 [768, 2048], P(('dp', 'sub'))
- rate_mean: float32 [], replicated
- rate_max: float32 [], replicated
Inputs may be any that keep to these rules, and one draw needn't show every extreme that they name: `seq_lengths`: row d lists, in order, the sequences packed into the 128 slots of device d (devices in dp-major order); each takes its length rounded up to a multiple of 16 slots, right after the previous one; a length of 0 takes no slots and the rounded lengths of a row sum to at most 128; the first length of every row is 1 or more; in every draw one device holds a single sequence of exactly 128 tokens.
All inputs are finite; a program needn't handle non-finite values.
Results may differ from a plain program's by a relative error of at most 0.0081.
Values may be sent and summed in bfloat16 or wider, within the bound.
A program may use at most 192 MiB of HBM per device.

v0:
```python
import jax
import jax.numpy as jnp
from jax import lax
from jax.sharding import PartitionSpec as P

HEADS = 12
HEAD = 64
MINI = 16


EPS = 1e-06
BASE_RATE = 1.0


def slot_layout(lengths, slot_total):
    padded = (lengths + (MINI - 1)) // MINI * MINI
    sequence_stops = jnp.cumsum(padded)
    seq_starts = sequence_stops - padded
    slot_ids = jnp.arange(slot_total, dtype=jnp.int32)
    inside = (slot_ids[:, None] >= seq_starts[None, :]) & (
        slot_ids[:, None] < seq_starts[None, :] + lengths[None, :]
    )
    slot_mask = jnp.max(inside.astype(jnp.float32), axis=1)
    batch_first = jnp.arange(slot_total // MINI, dtype=jnp.int32) * MINI
    opening = (batch_first[:, None] == seq_starts[None, :]) & (lengths[None, :] > 0)
    batch_open = jnp.max(opening.astype(jnp.float32), axis=1)
    return (slot_mask, batch_open)


def head_norm(values, gain_vec, bias_vec):
    centre = values - jnp.mean(values, axis=-1, keepdims=True)
    scaled = lax.rsqrt(jnp.mean(centre * centre, axis=-1, keepdims=True) + EPS)
    normed = centre * scaled
    return (normed * gain_vec + bias_vec, normed, scaled)


def inner_mixer(
    queries,
    key_rows,
    value_rows,
    rate_logit,
    slot_mask,
    batch_open,
    init_weight,
    init_bias,
    inner_gain,
    inner_bias,
):
    slot_total = queries.shape[0]
    batches = slot_total // MINI

    def heads_first(values):
        return values.reshape(batches, MINI, HEADS, HEAD).transpose(0, 2, 1, 3)

    rates = BASE_RATE / HEAD * jax.nn.sigmoid(rate_logit)
    rates = rates.reshape(batches, MINI, HEADS).transpose(0, 2, 1)
    weight_zero = init_weight.reshape(HEADS, HEAD, HEAD)
    bias_zero = init_bias.reshape(HEADS, HEAD)
    gain_heads = inner_gain.reshape(HEADS, 1, HEAD)
    shift_heads = inner_bias.reshape(HEADS, 1, HEAD)
    places = jnp.arange(MINI, dtype=jnp.float32)
    causal = (places[:, None] >= places[None, :]).astype(jnp.float32) / (places[:, None] + 1.0)
    precise_result = lax.Precision.HIGHEST

    def advance(carried, inputs_mb):
        current_weight, current_bias = carried
        query_mb, key_minibatch, value_mb, rate_mb, mask_mb, opening = inputs_mb
        current_weight = opening * weight_zero + (1.0 - opening) * current_weight
        current_bias = opening * bias_zero + (1.0 - opening) * current_bias
        inner_preactivation = (
            jnp.einsum("svf,sfl->svl", key_minibatch, current_weight, precision=precise_result)
            + current_bias[:, None, :]
        )
        rebuilt, normed, scaled = head_norm(inner_preactivation, gain_heads, shift_heads)
        error_term = gain_heads * (rebuilt - (value_mb - key_minibatch))
        grad_pre = scaled * (
            error_term
            - jnp.mean(error_term, axis=-1, keepdims=True)
            - normed * jnp.mean(error_term * normed, axis=-1, keepdims=True)
        )
        grad_pre = grad_pre * mask_mb[None, :, None]
        step_rates = causal[None] * rate_mb[:, None, :]
        scores = jnp.einsum("hid,hjd->hij", query_mb, key_minibatch, precision=precise_result) + 1.0
        updated = (
            jnp.einsum("hid,hde->hie", query_mb, current_weight, precision=precise_result)
            + current_bias[:, None, :]
            - jnp.einsum("hij,hje->hie", step_rates * scores, grad_pre, precision=precise_result)
        )
        answer, unused_a, unused_b = head_norm(updated, gain_heads, shift_heads)
        last_rates = rate_mb / MINI
        weight_next = current_weight - jnp.einsum(
            "hjd,hje->hde",
            key_minibatch * last_rates[:, :, None],
            grad_pre,
            precision=precise_result,
        )
        bias_next = current_bias - jnp.sum(last_rates[:, :, None] * grad_pre, axis=1)
        return ((weight_next, bias_next), query_mb + answer)

    initial = (jnp.zeros((HEADS, HEAD, HEAD), jnp.float32), jnp.zeros((HEADS, HEAD), jnp.float32))
    unused_state, outputs = lax.scan(
        advance,
        initial,
        (
            heads_first(queries),
            heads_first(key_rows),
            heads_first(value_rows),
            rates,
            slot_mask.reshape(batches, MINI),
            batch_open,
        ),
    )
    return outputs.transpose(0, 2, 1, 3).reshape(slot_total, HEADS * HEAD)


def rms_scale(values):
    return lax.rsqrt(jnp.mean(values * values, axis=-1, keepdims=True) + EPS)


def row_norm(values):
    centre = values - jnp.mean(values, axis=-1, keepdims=True)
    scaled = lax.rsqrt(jnp.mean(centre * centre, axis=-1, keepdims=True) + EPS)
    return (centre * scaled, scaled)


def contract_rows(left, right):
    return lax.dot_general(
        left, right, (((0,), (0,)), ((), ())), preferred_element_type=jnp.float32
    )


def contract_cols(left, right):
    return lax.dot_general(
        left, right, (((1,), (1,)), ((), ())), preferred_element_type=jnp.float32
    )


def per_device(
    tokens,
    cotangent,
    seq_lengths,
    norm_gain,
    weight_query,
    weight_key,
    weight_value,
    weight_rate,
    bias_rate,
    init_weight,
    init_bias,
    inner_gain,
    inner_bias,
    post_gain,
    post_bias,
    weight_out,
    mlp_gain,
    weight_gate,
    weight_up,
    weight_down,
):
    slot_total = tokens.shape[0]
    slot_mask, batch_open = slot_layout(seq_lengths[0], slot_total)
    mixer_full = (
        lax.all_gather(norm_gain, ("dp", "sub"), axis=0, tiled=True),
        lax.all_gather(weight_query, ("dp", "sub"), axis=0, tiled=True),
        lax.all_gather(weight_key, ("dp", "sub"), axis=0, tiled=True),
        lax.all_gather(weight_value, ("dp", "sub"), axis=0, tiled=True),
        lax.all_gather(weight_rate, ("dp", "sub"), axis=0, tiled=True),
        lax.all_gather(init_weight, ("dp", "sub"), axis=0, tiled=True),
        lax.all_gather(init_bias, ("dp", "sub"), axis=0, tiled=True),
        lax.all_gather(inner_gain, ("dp", "sub"), axis=0, tiled=True),
        lax.all_gather(inner_bias, ("dp", "sub"), axis=0, tiled=True),
        lax.all_gather(post_gain, ("dp", "sub"), axis=0, tiled=True),
        lax.all_gather(post_bias, ("dp", "sub"), axis=0, tiled=True),
        lax.all_gather(weight_out, ("dp", "sub"), axis=0, tiled=True),
    )
    mlp_full = (
        lax.all_gather(mlp_gain, ("dp", "sub"), axis=0, tiled=True),
        lax.all_gather(weight_gate, ("dp", "sub"), axis=0, tiled=True),
        lax.all_gather(weight_up, ("dp", "sub"), axis=0, tiled=True),
        lax.all_gather(weight_down, ("dp", "sub"), axis=0, tiled=True),
    )
    (
        first_gain,
        query_full,
        key_full,
        value_full,
        rate_full,
        init_full,
        init_bias_full,
        inner_gain_full,
        inner_bias_full,
        post_gain_full,
        post_bias_full,
        out_full,
    ) = mixer_full
    gain_two, gate_full, up_full, down_full = mlp_full
    inputs = tokens.astype(jnp.float32)
    scale_one = rms_scale(inputs)
    unit_one = inputs * scale_one
    normed = (unit_one * first_gain.astype(jnp.float32)).astype(jnp.bfloat16)
    queries = jnp.dot(normed, query_full, preferred_element_type=jnp.float32)
    key_rows = jnp.dot(normed, key_full, preferred_element_type=jnp.float32)
    value_rows = jnp.dot(normed, value_full, preferred_element_type=jnp.float32)
    rate_logit = jnp.dot(normed, rate_full, preferred_element_type=jnp.float32) + bias_rate.astype(
        jnp.float32
    )
    rates = BASE_RATE / HEAD * jax.nn.sigmoid(rate_logit)

    def mixer_local(query_in, key_in, value_in, logit_in, weight_in, bias_in, gain_in, shift_in):
        return inner_mixer(
            query_in,
            key_in,
            value_in,
            logit_in,
            slot_mask,
            batch_open,
            weight_in,
            bias_in,
            gain_in,
            shift_in,
        )

    mixed, mixer_pull = jax.vjp(
        mixer_local,
        queries,
        key_rows,
        value_rows,
        rate_logit,
        init_full.astype(jnp.float32),
        init_bias_full.astype(jnp.float32),
        inner_gain_full.astype(jnp.float32),
        inner_bias_full.astype(jnp.float32),
    )
    post_hat, post_scale = row_norm(mixed)
    post = (
        post_hat * post_gain_full.astype(jnp.float32) + post_bias_full.astype(jnp.float32)
    ).astype(jnp.bfloat16)
    branch = jnp.dot(post, out_full, preferred_element_type=jnp.float32)
    hidden = inputs + branch
    scale_two = rms_scale(hidden)
    unit_two = hidden * scale_two
    normed_two = (unit_two * gain_two.astype(jnp.float32)).astype(jnp.bfloat16)
    gate = jnp.dot(normed_two, gate_full, preferred_element_type=jnp.float32)
    up_proj = jnp.dot(normed_two, up_full, preferred_element_type=jnp.float32)
    sigmoid_gate = jax.nn.sigmoid(gate)
    silu_gate = gate * sigmoid_gate
    activ = (silu_gate * up_proj).astype(jnp.bfloat16)
    mlp_out = contract_cols(activ, down_full)
    result = (slot_mask[:, None] * (hidden + mlp_out)).astype(jnp.bfloat16)
    back_mixer = (
        lax.all_gather(norm_gain, ("dp", "sub"), axis=0, tiled=True),
        lax.all_gather(weight_query, ("dp", "sub"), axis=0, tiled=True),
        lax.all_gather(weight_key, ("dp", "sub"), axis=0, tiled=True),
        lax.all_gather(weight_value, ("dp", "sub"), axis=0, tiled=True),
        lax.all_gather(weight_rate, ("dp", "sub"), axis=0, tiled=True),
        lax.all_gather(init_weight, ("dp", "sub"), axis=0, tiled=True),
        lax.all_gather(init_bias, ("dp", "sub"), axis=0, tiled=True),
        lax.all_gather(inner_gain, ("dp", "sub"), axis=0, tiled=True),
        lax.all_gather(inner_bias, ("dp", "sub"), axis=0, tiled=True),
        lax.all_gather(post_gain, ("dp", "sub"), axis=0, tiled=True),
        lax.all_gather(post_bias, ("dp", "sub"), axis=0, tiled=True),
        lax.all_gather(weight_out, ("dp", "sub"), axis=0, tiled=True),
    )
    back_mlp = (
        lax.all_gather(mlp_gain, ("dp", "sub"), axis=0, tiled=True),
        lax.all_gather(weight_gate, ("dp", "sub"), axis=0, tiled=True),
        lax.all_gather(weight_up, ("dp", "sub"), axis=0, tiled=True),
        lax.all_gather(weight_down, ("dp", "sub"), axis=0, tiled=True),
    )
    gain_one_back = back_mixer[0].astype(jnp.float32)
    query_back, key_back, value_back, rate_back = (
        back_mixer[1],
        back_mixer[2],
        back_mixer[3],
        back_mixer[4],
    )
    post_gain_back = back_mixer[9].astype(jnp.float32)
    out_back = back_mixer[11]
    gain_two_back = back_mlp[0].astype(jnp.float32)
    gate_back, up_back, down_back = (back_mlp[1], back_mlp[2], back_mlp[3])
    masked_cot = cotangent.astype(jnp.float32) * slot_mask[:, None]
    mlp_cot = masked_cot.astype(jnp.bfloat16)
    grad_down = contract_rows(mlp_cot, activ)
    act_cot = jnp.dot(mlp_cot, down_back, preferred_element_type=jnp.float32)
    silu_slope = sigmoid_gate * (1.0 + gate * (1.0 - sigmoid_gate))
    gate_cot = (act_cot * up_proj * silu_slope).astype(jnp.bfloat16)
    up_cot = (act_cot * silu_gate).astype(jnp.bfloat16)
    grad_gate = contract_rows(normed_two, gate_cot)
    grad_up = contract_rows(normed_two, up_cot)
    two_cot = contract_cols(gate_cot, gate_back) + contract_cols(up_cot, up_back)
    grad_mlp_gain = jnp.sum(two_cot * unit_two, axis=0)
    unit_two_cot = two_cot * gain_two_back
    hidden_cot = masked_cot + scale_two * (
        unit_two_cot - unit_two * jnp.mean(unit_two_cot * unit_two, axis=-1, keepdims=True)
    )
    branch_cot = hidden_cot.astype(jnp.bfloat16)
    grad_out = contract_rows(post, branch_cot)
    post_cot = contract_cols(branch_cot, out_back)
    grad_post_gain = jnp.sum(post_cot * post_hat, axis=0)
    grad_post_bias = jnp.sum(post_cot, axis=0)
    hat_cot = post_cot * post_gain_back
    mixed_cot = post_scale * (
        hat_cot
        - jnp.mean(hat_cot, axis=-1, keepdims=True)
        - post_hat * jnp.mean(hat_cot * post_hat, axis=-1, keepdims=True)
    )
    (
        query_cot,
        key_cot,
        value_cot,
        logit_cot,
        grad_init_weight,
        grad_init_bias,
        grad_inner_gain,
        grad_inner_bias,
    ) = mixer_pull(mixed_cot)
    query_low = query_cot.astype(jnp.bfloat16)
    key_low = key_cot.astype(jnp.bfloat16)
    value_low = value_cot.astype(jnp.bfloat16)
    logit_low = logit_cot.astype(jnp.bfloat16)
    grad_query = contract_rows(normed, query_low)
    grad_key = contract_rows(normed, key_low)
    grad_value = contract_rows(normed, value_low)
    grad_rate = contract_rows(normed, logit_low)
    grad_bias_local = jnp.sum(logit_low.astype(jnp.float32), axis=0)
    one_cot = (
        contract_cols(query_low, query_back)
        + contract_cols(key_low, key_back)
        + contract_cols(value_low, value_back)
        + contract_cols(logit_low, rate_back)
    )
    grad_norm_gain = jnp.sum(one_cot * unit_one, axis=0)
    unit_one_cot = one_cot * gain_one_back
    input_cot = hidden_cot + scale_one * (
        unit_one_cot - unit_one * jnp.mean(unit_one_cot * unit_one, axis=-1, keepdims=True)
    )
    grad_tokens = input_cot.astype(jnp.bfloat16)
    mixer_grads = (
        lax.psum_scatter(grad_norm_gain, ("dp", "sub"), scatter_dimension=0, tiled=True),
        lax.psum_scatter(grad_query, ("dp", "sub"), scatter_dimension=0, tiled=True),
        lax.psum_scatter(grad_key, ("dp", "sub"), scatter_dimension=0, tiled=True),
        lax.psum_scatter(grad_value, ("dp", "sub"), scatter_dimension=0, tiled=True),
        lax.psum_scatter(grad_rate, ("dp", "sub"), scatter_dimension=0, tiled=True),
        lax.psum_scatter(grad_init_weight, ("dp", "sub"), scatter_dimension=0, tiled=True),
        lax.psum_scatter(grad_init_bias, ("dp", "sub"), scatter_dimension=0, tiled=True),
        lax.psum_scatter(grad_inner_gain, ("dp", "sub"), scatter_dimension=0, tiled=True),
        lax.psum_scatter(grad_inner_bias, ("dp", "sub"), scatter_dimension=0, tiled=True),
        lax.psum_scatter(grad_post_gain, ("dp", "sub"), scatter_dimension=0, tiled=True),
        lax.psum_scatter(grad_post_bias, ("dp", "sub"), scatter_dimension=0, tiled=True),
        lax.psum_scatter(grad_out, ("dp", "sub"), scatter_dimension=0, tiled=True),
    )
    mlp_grads = (
        lax.psum_scatter(grad_mlp_gain, ("dp", "sub"), scatter_dimension=0, tiled=True),
        lax.psum_scatter(grad_gate, ("dp", "sub"), scatter_dimension=0, tiled=True),
        lax.psum_scatter(grad_up, ("dp", "sub"), scatter_dimension=0, tiled=True),
        lax.psum_scatter(grad_down, ("dp", "sub"), scatter_dimension=0, tiled=True),
    )
    live_rates = slot_mask[:, None] * rates
    rate_total, rate_count, grad_bias_rate = lax.psum(
        (jnp.sum(live_rates), jnp.sum(slot_mask) * HEADS, grad_bias_local), ("dp", "sub")
    )
    rate_peak = lax.pmax(jnp.max(live_rates), ("dp", "sub"))
    return (
        result,
        grad_tokens,
        mixer_grads[0],
        mixer_grads[1],
        mixer_grads[2],
        mixer_grads[3],
        mixer_grads[4],
        grad_bias_rate,
        mixer_grads[5],
        mixer_grads[6],
        mixer_grads[7],
        mixer_grads[8],
        mixer_grads[9],
        mixer_grads[10],
        mixer_grads[11],
        mlp_grads[0],
        mlp_grads[1],
        mlp_grads[2],
        mlp_grads[3],
        rate_total / rate_count,
        rate_peak,
    )


def solution(mesh):
    return jax.shard_map(
        per_device,
        mesh=mesh,
        in_specs=(
            P(("dp", "sub"), None),
            P(("dp", "sub"), None),
            P(("dp", "sub"), None),
            P(("dp", "sub")),
            P(("dp", "sub"), None),
            P(("dp", "sub"), None),
            P(("dp", "sub"), None),
            P(("dp", "sub"), None),
            P(),
            P(("dp", "sub"), None),
            P(("dp", "sub")),
            P(("dp", "sub")),
            P(("dp", "sub")),
            P(("dp", "sub")),
            P(("dp", "sub")),
            P(("dp", "sub"), None),
            P(("dp", "sub")),
            P(("dp", "sub"), None),
            P(("dp", "sub"), None),
            P(("dp", "sub"), None),
        ),
        out_specs=(
            P(("dp", "sub"), None),
            P(("dp", "sub"), None),
            P(("dp", "sub")),
            P(("dp", "sub"), None),
            P(("dp", "sub"), None),
            P(("dp", "sub"), None),
            P(("dp", "sub"), None),
            P(),
            P(("dp", "sub"), None),
            P(("dp", "sub")),
            P(("dp", "sub")),
            P(("dp", "sub")),
            P(("dp", "sub")),
            P(("dp", "sub")),
            P(("dp", "sub"), None),
            P(("dp", "sub")),
            P(("dp", "sub"), None),
            P(("dp", "sub"), None),
            P(("dp", "sub"), None),
            P(),
            P(),
        ),
        check_vma=False,
    )
```

profile of v0, /device:TPU:1, one launch (start us, length us, event | category | flops | bytes accessed | tf_op | source)
XLA Modules:
  0.0 3855.2 jit_solution(8462524711750314241)
XLA Ops:
  21.5 69.1 %all-reduce.31 = (bf16[768]{0:T(1024)(128)(2,1)S(1)}, bf16[768]{0:T(1024)(128)(2,1)S(1)}, bf16[768]{0:T(1024)(128)(2,1)S(1)}, bf16[768]{0:T(1024)(128)(2,1)S(1)}...) all-reduce(bf16[768]{0:T(1024)(128)(2,1)S(1)} %dynamic-update-slice, ...), channel_id=1, replica_groups=mesh['dp'=16,'sub'=8] {'dp','sub'}, use_global_device_ids=true, to_apply=%add | all-reduce | flops 5376 | bytes 21504
  91.6 297.6 %all-gather.2 = bf16[128,6,12]{2,1,0:T(8,128)(2,1)S(1)} all-gather(bf16[1,6,12]{2,1,0:T(8,128)(2,1)} %bitcast.432), channel_id=1, replica_groups=mesh['dp'=16,'sub'=8] {'dp','sub'}, dimensions={0}, use_global_device_ids=true | all-gather | bytes 18576 | tf_op jit(solution)/shard_map/all_gather | solution.py:167
  392.2 311.6 %all-gather = bf16[128,6,64]{2,1,0:T(8,128)(2,1)S(1)} all-gather(bf16[1,6,64]{2,1,0:T(8,128)(2,1)S(1)} %bitcast.433), channel_id=1, replica_groups=mesh['dp'=16,'sub'=8] {'dp','sub'}, dimensions={0}, use_global_device_ids=true | all-gather | bytes 99072 | tf_op jit(solution)/shard_map/all_gather | solution.py:168
  718.8 193.1 %all-gather.19.cloned.1.call-done = bf16[128,6,768]{2,1,0:T(8,128)(2,1)} async-done(((bf16[1,6,768]{2,1,0:T(8,128)(2,1)}), bf16[128,6,768]{2,1,0:T(8,128)(2,1)}) %all-gather.19.cloned.1.call-update) | async-done | bytes 1179664 | tf_op jit(solution)/shard_map/all_gather | solution.py:166
  929.1 147.2 %while.96 = (s32[]{:T(128)}, f32[12,64,64]{2,1,0:T(8,128)}, f32[12,64]{1,0:T(8,128)S(1)}, f32[8,12,16,64]{3,2,1,0:T(8,128)S(1)}, f32[8]{0:T(128)}, /*index=5*/f3...) while((s32[]{:T(128)}, f32[12,64,64]{2,1,0:T(8,128)}, ...), condition=%wide.region_12.13_spmd.clone.clone, body=%wide.region_4.12_spmd.clone.clone.sunk | while | flops 33878212 | bytes 5858412 | solution.py:101
  1079.7 131.8 %all-gather.23.cloned.1.call-done = bf16[128,6,768]{2,1,0:T(8,128)(2,1)} async-done(((bf16[1,6,768]{2,1,0:T(8,128)(2,1)}), bf16[128,6,768]{2,1,0:T(8,128)(2,1)}) %all-gather.23.cloned.1.call-update) | async-done | bytes 1179664 | tf_op jit(solution)/shard_map/all_gather | solution.py:174
  1217.3 302.1 %all-gather.25.cloned.1.call-done = bf16[128,6,2048]{2,1,0:T(8,128)(2,1)} async-done(((bf16[1,6,2048]{2,1,0:T(8,128)(2,1)}), bf16[128,6,2048]{2,1,0:T(8,128)(2,1)}) %all-gather.25.cloned.1.call-update) | async-done | bytes 3145744 | tf_op jit(solution)/shard_map/all_gather | solution.py:178
  1525.7 302.9 %all-gather.27.cloned.1.call-done = bf16[128,6,2048]{2,1,0:T(8,128)(2,1)} async-done(((bf16[1,6,2048]{2,1,0:T(8,128)(2,1)}), bf16[128,6,2048]{2,1,0:T(8,128)(2,1)}) %all-gather.27.cloned.1.call-update) | async-done | bytes 3145744 | tf_op jit(solution)/shard_map/all_gather | solution.py:179
  1838.6 299.3 %all-gather.29.cloned.1.call-done = bf16[128,6,2048]{2,1,0:T(8,128)(2,1)} async-done(((bf16[1,6,2048]{2,1,0:T(8,128)(2,1)}), bf16[128,6,2048]{2,1,0:T(8,128)(2,1)}) %all-gather.29.cloned.1.call-update) | async-done | bytes 3145744 | tf_op jit(solution)/shard_map/all_gather | solution.py:180
  2164.1 260.4 %while.95 = (s32[]{:T(128)}, f32[12,64,64]{2,1,0:T(8,128)S(1)}, f32[12,64]{1,0:T(8,128)S(1)}, f32[12,1,64]{2,1,0:T(1,128)S(1)}, f32[12,1,64]{2,1,0:T(1,128)S(1)}...) while((s32[]{:T(128)}, f32[12,64,64]{2,1,0:T(8,128)S(1)}, ...), condition=%wide.region_37.38_spmd.clone, body=%wide.region_19.37_spmd.clone.sunk | while | flops 67509696 | bytes 6398689 | solution.py:101
  2436.7 446.1 %fusion.171 = (f32[8,768]{1,0:T(8,128)}, f32[8,768]{1,0:T(8,128)}, f32[8,768]{1,0:T(8,128)}, f32[8,768]{1,0:T(8,128)}, f32[8,2048]{1,0:T(8,128)}, /*index=5*/f32[8,2048]{1,0:T(8,128)}, f32[8,2048]{1,0:T(8,128)}) fusion(f32[768,768]{1,0:T(8,128)} %fusion.162, f32[768,768]{1,0:T(8,128)} %fusion.160, f32[768,768]{1,0:T(8,128)} %fusion.158, ...), kind=kCustom, calls=%all-reduce-scatter.7 | all-reduce-scatter fusion | flops 9437185 | bytes 28606464
  2883.5 14.7 collective-permute-start.127
  2988.0 10.2 collective-permute-start.97
  2998.2 10.2 collective-permute-start.98
  3008.4 10.2 collective-permute-start.99
  3407.4 67.7 %all-reduce.30 = (f32[768]{0:T(1024)S(1)}, f32[768,12]{1,0:T(8,128)S(1)}, f32[12]{0:T(128)}, f32[768]{0:T(1024)S(1)}, f32[768]{0:T(1024)S(1)}, /*index=5*/f32[76...) all-reduce(f32[768]{0:T(1024)S(1)} %get-tuple-element.1750, ...), channel_id=2, replica_groups=mesh['dp'=16,'sub'=8] {'dp','sub'}, use_global_device_ids=true, to_apply=%region_40.41.clone | all-reduce | flops 14606 | bytes 116848
  3498.4 65.5 %pmax.7 = f32[]{:T(128)} all-reduce(f32[]{:T(128)} %get-tuple-element.1754), channel_id=1, replica_groups=mesh['dp'=16,'sub'=8] {'dp','sub'}, use_global_device_ids=true, to_apply=%region_66.67 | all-reduce | flops 1 | bytes 8 | tf_op jit(solution)/shard_map/pmax | solution.py:362
  3583.3 27.2 concatenate.3
  3610.6 27.2 concatenate.2
  3637.8 27.2 concatenate.1
  3665.1 27.2 concatenate
  3754.5 29.4 concatenate.6
  3794.3 18.4 concatenate.5
  3820.7 24.3 concatenate.4
  (1630 shorter events, 1111.9 us)
Async XLA Ops:
  7.2 698.5 %all-gather.17.cloned.1.call-start = ((), (), s32[]{:S(2)}) async-start(), calls=%async_computation | async-start | bytes 1585152 | tf_op jit(solution)/shard_map/all_gather | solution.py:165
  8.0 703.2 %all-gather.21.cloned.1.call-start = ((), (), s32[]{:S(2)}) async-start(), calls=%async_computation.2 | async-start | bytes 1585152 | tf_op jit(solution)/shard_map/all_gather | solution.py:164
  8.7 903.2 %all-gather.19.cloned.1.call-start = ((), (), s32[]{:S(2)}) async-start(), calls=%async_computation.1 | async-start | bytes 1585152 | tf_op jit(solution)/shard_map/all_gather | solution.py:166
  9.5 1202.0 %all-gather.23.cloned.1.call-start = ((), (), s32[]{:S(2)}) async-start(), calls=%async_computation.3 | async-start | bytes 1585152 | tf_op jit(solution)/shard_map/all_gather | solution.py:174
  10.0 1509.3 %all-gather.25.cloned.1.call-start = ((), (), s32[]{:S(2)}) async-start(), calls=%async_computation.4 | async-start | bytes 4227072 | tf_op jit(solution)/shard_map/all_gather | solution.py:178
  10.6 1818.0 %all-gather.27.cloned.1.call-start = ((), (), s32[]{:S(2)}) async-start(), calls=%async_computation.5 | async-start | bytes 4227072 | tf_op jit(solution)/shard_map/all_gather | solution.py:179
  11.2 2126.7 %all-gather.29.cloned.1.call-start = ((), (), s32[]{:S(2)}) async-start(), calls=%async_computation.6 | async-start | bytes 4227072 | tf_op jit(solution)/shard_map/all_gather | solution.py:180
  11.9 3833.7 %all-reduce.35.cloned.1.call-start = ((), (), s32[]{:S(2)}) async-start(), calls=%async_computation.7 | async-start | bytes 786432
  3396.8 82.5 %collective-permute-start.177 = (f32[8,2048]{1,0:T(8,128)}, f32[8,2048]{1,0:T(8,128)S(1)}, u32[]{:S(2)}, u32[]{:S(2)}) collective-permute-start(f32[8,2048]{1,0:T(8,128)} %get-tuple-element.1934), channel_id=1, source_target_pairs={{0,18},{1,19},{2,20},{3,21},{4,22},{5,23},{6,24},{7,25},{8,26},{9,... | collective-permute-start | bytes 196616
  3400.3 83.6 %collective-permute-start.178 = (f32[8,2048]{1,0:T(8,128)}, f32[8,2048]{1,0:T(8,128)S(1)}, u32[]{:S(2)}, u32[]{:S(2)}) collective-permute-start(f32[8,2048]{1,0:T(8,128)} %get-tuple-element.1934), channel_id=1, source_target_pairs={{0,19},{1,20},{2,21},{3,22},{4,23},{5,24},{6,25},{7,26},{8,27},{9,... | collective-permute-start | bytes 196616
  3402.2 83.0 %collective-permute-start.179 = (f32[8,2048]{1,0:T(8,128)}, f32[8,2048]{1,0:T(8,128)S(1)}, u32[]{:S(2)}, u32[]{:S(2)}) collective-permute-start(f32[8,2048]{1,0:T(8,128)} %get-tuple-element.1934), channel_id=1, source_target_pairs={{0,20},{1,21},{2,22},{3,23},{4,24},{5,25},{6,26},{7,27},{8,28},{9,... | collective-permute-start | bytes 196616
  3403.5 84.4 %collective-permute-start.180 = (f32[8,2048]{1,0:T(8,128)}, f32[8,2048]{1,0:T(8,128)S(1)}, u32[]{:S(2)}, u32[]{:S(2)}) collective-permute-start(f32[8,2048]{1,0:T(8,128)} %get-tuple-element.1934), channel_id=1, source_target_pairs={{0,21},{1,22},{2,23},{3,24},{4,25},{5,26},{6,27},{7,28},{8,29},{9,... | collective-permute-start | bytes 196616
  3404.8 90.1 %collective-permute-start.181 = (f32[8,2048]{1,0:T(8,128)}, f32[8,2048]{1,0:T(8,128)S(1)}, u32[]{:S(2)}, u32[]{:S(2)}) collective-permute-start(f32[8,2048]{1,0:T(8,128)} %get-tuple-element.1934), channel_id=1, source_target_pairs={{0,22},{1,23},{2,24},{3,25},{4,26},{5,27},{6,28},{7,29},{8,30},{9,... | collective-permute-start | bytes 196616
  3479.3 85.9 %collective-permute-start.182 = (f32[8,2048]{1,0:T(8,128)}, f32[8,2048]{1,0:T(8,128)S(1)}, u32[]{:S(2)}, u32[]{:S(2)}) collective-permute-start(f32[8,2048]{1,0:T(8,128)} %get-tuple-element.1934), channel_id=1, source_target_pairs={{0,23},{1,24},{2,25},{3,26},{4,27},{5,28},{6,29},{7,30},{8,31},{9,... | collective-permute-start | bytes 196616
  3483.9 84.3 %collective-permute-start.183 = (f32[8,2048]{1,0:T(8,128)}, f32[8,2048]{1,0:T(8,128)S(1)}, u32[]{:S(2)}, u32[]{:S(2)}) collective-permute-start(f32[8,2048]{1,0:T(8,128)} %get-tuple-element.1934), channel_id=1, source_target_pairs={{0,24},{1,25},{2,26},{3,27},{4,28},{5,29},{6,30},{7,31},{8,32},{9,... | collective-permute-start | bytes 196616
  3485.2 85.9 %collective-permute-start.184 = (f32[8,2048]{1,0:T(8,128)}, f32[8,2048]{1,0:T(8,128)S(1)}, u32[]{:S(2)}, u32[]{:S(2)}) collective-permute-start(f32[8,2048]{1,0:T(8,128)} %get-tuple-element.1934), channel_id=1, source_target_pairs={{0,25},{1,26},{2,27},{3,28},{4,29},{5,30},{6,31},{7,32},{8,33},{9,... | collective-permute-start | bytes 196616
  3487.9 88.2 %collective-permute-start.185 = (f32[8,2048]{1,0:T(8,128)}, f32[8,2048]{1,0:T(8,128)S(1)}, u32[]{:S(2)}, u32[]{:S(2)}) collective-permute-start(f32[8,2048]{1,0:T(8,128)} %get-tuple-element.1934), channel_id=1, source_target_pairs={{0,26},{1,27},{2,28},{3,29},{4,30},{5,31},{6,32},{7,33},{8,34},{9,... | collective-permute-start | bytes 196616
  3494.9 85.3 %collective-permute-start.186 = (f32[8,2048]{1,0:T(8,128)}, f32[8,2048]{1,0:T(8,128)S(1)}, u32[]{:S(2)}, u32[]{:S(2)}) collective-permute-start(f32[8,2048]{1,0:T(8,128)} %get-tuple-element.1934), channel_id=1, source_target_pairs={{0,27},{1,28},{2,29},{3,30},{4,31},{5,32},{6,33},{7,34},{8,35},{9,... | collective-permute-start | bytes 196616
  3565.2 127.1 %collective-permute-start.187 = (f32[8,2048]{1,0:T(8,128)}, f32[8,2048]{1,0:T(8,128)}, u32[]{:S(2)}, u32[]{:S(2)}) collective-permute-start(f32[8,2048]{1,0:T(8,128)} %get-tuple-element.1934), channel_id=1, source_target_pairs={{0,28},{1,29},{2,30},{3,31},{4,32},{5,33},{6,34},{7,35},{8,36},{9,... | collective-permute-start | bytes 196616
  3568.2 126.3 %collective-permute-start.188 = (f32[8,2048]{1,0:T(8,128)}, f32[8,2048]{1,0:T(8,128)}, u32[]{:S(2)}, u32[]{:S(2)}) collective-permute-start(f32[8,2048]{1,0:T(8,128)} %get-tuple-element.1934), channel_id=1, source_target_pairs={{0,29},{1,30},{2,31},{3,32},{4,33},{5,34},{6,35},{7,36},{8,37},{9,... | collective-permute-start | bytes 196616
  3571.2 127.3 %collective-permute-start.189 = (f32[8,2048]{1,0:T(8,128)}, f32[8,2048]{1,0:T(8,128)}, u32[]{:S(2)}, u32[]{:S(2)}) collective-permute-start(f32[8,2048]{1,0:T(8,128)} %get-tuple-element.1934), channel_id=1, source_target_pairs={{0,30},{1,31},{2,32},{3,33},{4,34},{5,35},{6,36},{7,37},{8,38},{9,... | collective-permute-start | bytes 196616
  3576.2 124.7 %collective-permute-start.190 = (f32[8,2048]{1,0:T(8,128)}, f32[8,2048]{1,0:T(8,128)}, u32[]{:S(2)}, u32[]{:S(2)}) collective-permute-start(f32[8,2048]{1,0:T(8,128)} %get-tuple-element.1934), channel_id=1, source_target_pairs={{0,31},{1,32},{2,33},{3,34},{4,35},{5,36},{6,37},{7,38},{8,39},{9,... | collective-permute-start | bytes 196616
  3580.3 123.7 %collective-permute-start.128 = (f32[8,2048]{1,0:T(8,128)S(1)}, f32[8,2048]{1,0:T(8,128)}, u32[]{:S(2)}, u32[]{:S(2)}) collective-permute-start(f32[8,2048]{1,0:T(8,128)S(1)} %copy-done.33), channel_id=1, source_target_pairs={{0,1},{1,2},{2,3},{3,4},{4,5},{5,6},{6,7},{7,8},{8,9},{9,10},{10,1... | collective-permute-start | bytes 196616
  3741.8 42.1 %collective-permute-start.144 = (f32[8,2048]{1,0:T(8,128)S(1)}, f32[8,2048]{1,0:T(8,128)}, u32[]{:S(2)}, u32[]{:S(2)}) collective-permute-start(f32[8,2048]{1,0:T(8,128)S(1)} %copy-done.33), channel_id=1, source_target_pairs={{0,17},{1,18},{2,19},{3,20},{4,21},{5,22},{6,23},{7,24},{8,25},{9,... | collective-permute-start | bytes 196616
  (445 other events, 30337.5 us)
Sparse Core Ops, SparseCore 0:
  9.8 300.9 all-gather.16
  312.5 298.8 all-gather.20
  613.1 298.8 all-gather.18
  913.5 297.8 all-gather.22
  1213.0 306.3 all-gather.24
  1520.9 307.6 all-gather.26
  1830.3 307.6 all-gather.28
  3479.4 141.6 all-reduce.34
where the time goes:
time: 3890 us; the launch traced here: 3860 us
  blocking collectives  1260 us (32%)
  waiting for transfers between devices  1230 us (32%)
  starting transfers between devices  618 us (16%)
  local copies, waits for them, and re-layouts  328 us (8%)
  matrix products  217 us (6%)
  other arithmetic  169 us (4%)
    unnamed x225, starting transfers between devices  617 us
    unnamed x3, blocking collectives  583 us
    all_gather x1, blocking collectives, per_device(): lax.all_gather(init_weight, ('dp', 'sub'), axis=0, tiled=True)  312 us
    all_gather x1, waiting for transfers between devices, per_device(): lax.all_gather(weight_up, ('dp', 'sub'), axis=0, tiled=True)  303 us
    all_gather x1, waiting for transfers between devices, per_device(): lax.all_gather(weight_gate, ('dp', 'sub'), axis=0, tiled=True)  302 us
    all_gather x1, waiting for transfers between devices, per_device(): lax.all_gather(weight_down, ('dp', 'sub'), axis=0, tiled=True)  299 us
    all_gather x1, blocking collectives, per_device(): lax.all_gather(weight_rate, ('dp', 'sub'), axis=0, tiled=True)  298 us
    unnamed x484, local copies, waits for them, and re-layouts  241 us
  transfers between devices with their start and end apart: 232, of which 6 were waited for; matrix products, arithmetic and copies ran while one was open for 11% of the time, Pallas kernels for 0%

commit v1 on v0

v1 whole, which is shorter than its diff:
```python
import jax
import jax.numpy as jnp
from jax import lax
from jax.experimental import pallas as pl
from jax.experimental.pallas import tpu as pltpu
from jax.sharding import PartitionSpec as P

MESH = pl.DeviceIdType.MESH
HEADS = 12
HEAD = 64
MINI = 16
EPS = 1e-06
F32 = jnp.float32
BF16 = jnp.bfloat16
S = 128
D = 768
FF = 2048
GROUPS = 3
RATE0 = 64
VEC0 = 76
ALL = slice(None)


class Wave:
    def __init__(self, base, nx, nz, ny, split=False):
        self.base, self.nx, self.nz, self.ny = base, nx, nz, ny
        self.half = 2 * nx + 2 * nz + 8 * ny
        self.per = nx + nz + ny
        self.split = split

    def start(self, h):
        return self.base if self.split else self.base + h * self.half

    def tx(self, h, xl):
        return self.start(h) + xl * self.nx

    def tz(self, h, xl):
        return self.start(h) + 2 * self.nx + xl * self.nz

    def ty(self, h, y, xl):
        return self.start(h) + 2 * self.nx + 2 * self.nz + (y * 2 + xl) * self.ny

    def mine(self, h, xl, y):
        return (
            [self.tx(h, xl) + n for n in range(self.nx)]
            + [self.tz(h, xl) + n for n in range(self.nz)]
            + [self.ty(h, y, xl) + n for n in range(self.ny)]
        )

    def span(self, color):
        return {
            "x": (0, 2 * self.nx),
            "z": (2 * self.nx, 2 * self.nz),
            "y": (2 * self.nx + 2 * self.nz, 8 * self.ny),
        }[color]

    def chain(self, color, me):
        if color == "x":
            return [
                ("z", lambda p: (self.tx(me.c, me.xl), self.nx, p, me.xh)),
                ("x", lambda p: (self.tx(me.c, p % 2), self.nx, ALL, p // 2)),
            ]
        if color == "z":
            return [
                ("x", lambda p: (self.tz(me.c, p % 2), self.nz, me.z, p // 2)),
                ("z", lambda p: (self.tz(me.c, 0), 2 * self.nz, p, ALL)),
            ]
        return [
            ("z", lambda p: (self.ty(me.c, me.y, me.xl), self.ny, p, me.xh)),
            ("x", lambda p: (self.ty(me.c, me.y, p % 2), self.ny, ALL, p // 2)),
            ("y", lambda p: (self.ty(me.c, p, 0), 2 * self.ny, ALL, ALL)),
        ]

    def colors(self, order="xzy"):
        return [k for k in order if {"x": self.nx, "z": self.nz, "y": self.ny}[k]]


ONE, THREE, TWO = Wave(0, 3, 3, 0), Wave(24, 1, 0, 0), Wave(28, 4, 4, 1, split=True)
OUT_WAVES = (ONE, THREE, TWO)
LAST, MID, FIRST = Wave(0, 2, 2, 0), Wave(16, 2, 1, 0), Wave(28, 4, 4, 1, split=True)
BACK_WAVES = (LAST, MID, FIRST)
TILES = 52
PER = max(sum(w.per for w in ws) for ws in (OUT_WAVES, BACK_WAVES))
PROWS = (PER * 6 + 15) // 16 * 16
TQ, TK, TS, TV = 0, 6, 12, 16
PADS = (25, 26, 27)
A_Q, A_K, A_V, A_O, A_G, A_U, A_D, A_S = range(8)
WIDTHS = (768, 768, 768, 768, 2048, 2048, 2048, 128)


def tile_out(c):
    return 13 + c if c < 3 else 19 + c


def tile_mlp(j, kind):
    return TWO.base + 6 * j + 2 * kind


def tile_source(w, h, t):
    if w.split:
        o = t - w.base
        return A_G + o % 6 // 2, 8 * h + o // 6 * 2 + o % 2
    if t in PADS:
        return None
    for a, first in ((A_Q, TQ), (A_K, TK), (A_V, TV)):
        if first <= t < first + 6:
            return a, t - first
    if t == TS:
        return A_S, 0
    return A_O, t - 13 if t < TV else t - 19


def nn(a, b):
    return lax.dot_general(a, b, (((1,), (0,)), ((), ())), preferred_element_type=F32)


def nt(a, b):
    return lax.dot_general(a, b, (((1,), (1,)), ((), ())), preferred_element_type=F32)


def tn(a, b):
    return lax.dot_general(a, b, (((0,), (0,)), ((), ())), preferred_element_type=F32)


def tt(a, b):
    return lax.dot_general(a, b, (((0,), (1,)), ((), ())), preferred_element_type=F32)


def iota(shape, dim):
    return lax.broadcasted_iota(jnp.int32, shape, dim)


def one_hot(cond):
    return jnp.where(cond, 1.0, 0.0).astype(BF16)


def split2(x):
    hi = x.astype(BF16)
    return hi, (x - hi.astype(F32)).astype(BF16)


def head_select(x, h):
    return jnp.where(iota(x.shape, 1) // HEAD == h, x, jnp.zeros_like(x))


def block_rows(x):
    return jnp.concatenate([head_select(x, h) for h in range(4)], axis=0)


def lanes(g):
    return pl.ds(256 * g, 256)


def layout_rows(lens_ref, token):
    mask = jnp.zeros(token.shape, F32)
    seg = jnp.zeros(token.shape, F32)
    start = jnp.int32(0)
    for j in range(4):
        n = lens_ref[0, j]
        mask += jnp.where((token >= start) & (token < start + n), 1.0, 0.0)
        seg += jnp.where((token >= start) & (n > 0), 1.0, 0.0)
        start += (n + 15) // 16 * 16
    return mask, seg


class Place:
    def __init__(self):
        dp, sub = lax.axis_index("dp"), lax.axis_index("sub")
        self.z = dp // 4
        self.xh = dp // 2 % 2
        self.c = dp % 2
        self.xl = sub // 4
        self.y = sub % 4
        self.x = self.xh * 2 + self.xl
        self.s = self.c * 8 + sub
        self.zx = self.z * 2 + self.xh

    def dev(self, z=None, x=None, y=None, c=None):
        z = self.z if z is None else z
        x = self.x if x is None else x
        y = self.y if y is None else y
        c = self.c if c is None else c
        return (z * 4 + x // 2 * 2 + c, x % 2 * 4 + y)

    def coord(self, axis):
        return getattr(self, axis)

    def step(self, axis, d):
        return self.dev(**{axis: (self.coord(axis) + d) % 4})

    def peer(self, dc, dxl, dy):
        c, xl, y = (self.c + dc) % 2, (self.xl + dxl) % 2, (self.y + dy) % 4
        return self.dev(x=self.xh * 2 + xl, y=y, c=c), c * 8 + xl * 4 + y

    def far(self, dz, dxh):
        return self.dev(z=(self.z + dz) % 4, x=(self.xh + dxh) % 2 * 2 + self.xl)


PEERS = tuple((dc, dxl, dy) for dc in range(2) for dxl in range(2) for dy in range(4) if (dc, dxl, dy) != (0, 0, 0))
FARS = tuple((dz, dxh) for dz in range(4) for dxh in range(2) if (dz, dxh) != (0, 0))


def blocks(rect):
    t, n, z, xh = rect
    nz, nxh = (4 if z is ALL else 1), (2 if xh is ALL else 1)

    def at(b):
        return (t + b // (nz * nxh), b // nxh % nz if z is ALL else z, b % nxh if xh is ALL else xh)

    return n * nz * nxh, at


def back_slots():
    slots = 0
    for w in BACK_WAVES:
        for color in w.colors():
            for _, rect in w.chain(color, Zero):
                slots += 3 * blocks(rect(0))[0]
    return slots


class Zero:
    z = xh = c = xl = y = x = s = 0


BACK_SLOTS = back_slots()
COPIES = sum((len(w.chain(k, Zero)) * 8 + 2) for w in OUT_WAVES + BACK_WAVES for k in w.colors()) + 3 * len(PEERS) + len(FARS) + 8


def view(ref, rect, half=None):
    t, n, z, xh = rect
    rows = ALL if half is None else pl.ds(48 * half, 48)
    return ref.at[pl.ds(t, n), z, xh, rows]


def f32(*shape):
    return pltpu.VMEM(shape, F32)


def b16(*shape):
    return pltpu.VMEM(shape, BF16)


INPUTS = ("norm_gain", "init_bias", "inner_gain", "inner_bias", "post_gain", "post_bias", "mlp_gain", "bias_rate", "tok", "cot",
          "wq", "wk", "wv", "wo", "wg", "wu", "wd", "init", "rate")
SCRATCH = dict(
    norm_gain=b16(1, 6), init_bias=b16(1, 6), inner_gain=b16(1, 6), inner_bias=b16(1, 6), post_gain=b16(1, 6), post_bias=b16(1, 6),
    mlp_gain=b16(1, 6), bias_rate=b16(1, HEADS), tok=b16(S, D), cot=b16(S, D), wq=b16(6, 768), wk=b16(6, 768), wv=b16(6, 768),
    wo=b16(6, 768), wg=b16(6, FF), wu=b16(6, FF), wd=b16(6, FF), init=b16(6, HEAD), rate=b16(6, HEADS), small=f32(6, 128),
    w4=b16(TILES, 4, 2, 96, 128), g4=b16(TILES, 4, 2, 96, 128), rc=b16(LAST.half + MID.half, 4, 2, 96, 128),
    land=b16(BACK_SLOTS, 96, 128), pk=b16(16, PROWS, 128), pkf=f32(16, PROWS, 128), rv=b16(16, PROWS, 128),
    rv2=b16(16, PROWS, 128), stf=f32(96, 128), sa=f32(16, 8, 128), sb=f32(8, 8, 128), stat=f32(8, 128), stat_sum=f32(8, 128),
    nrm=b16(S, D), q=f32(S, D), k=f32(S, D), v=f32(S, D), zc=f32(S, D), zq=f32(S, D), u=f32(S, D), gh=b16(S, D), gl=b16(S, D),
    s1=f32(S, D), c1=f32(S, D), e1=f32(S, D), y1=f32(S, D), n1=f32(S, D), n2=f32(S, D), s2=f32(S, D),
    mix=f32(S, D), hid=f32(S, D), post=b16(S, D), dzb=b16(S, D), dzc=b16(S, D), dgr=f32(S, D), dzf=f32(S, D),
    kbd=b16(GROUPS, 512, 256), qbd=b16(GROUPS, 512, 256), gbd=b16(GROUPS, 512, 256), dbd=b16(GROUPS, 512, 256),
    zbd=b16(GROUPS, 512, 256), pm=b16(GROUPS, S, 512), pmt=b16(GROUPS, S, 512), skk=f32(GROUPS, S, 512), sqk=f32(GROUPS, S, 512),
    rr=f32(GROUPS, S, 512), pscale=f32(S, 128), hcot=f32(S, D), bcot=b16(S, D), tcot=f32(S, D), ot=f32(S, D), out=b16(S, D),
    gtok=b16(S, D),
    nrm2=b16(2, S, D), mcot=b16(2, S, D), xt=b16(2, D, 2 * S), t2=f32(2, S, D), o2=f32(2, S, D), t_in=f32(S, D), o_in=f32(S, D),
    lsem=pltpu.SemaphoreType.DMA((len(INPUTS),)), ssem=pltpu.SemaphoreType.DMA((COPIES,)), rsem=pltpu.SemaphoreType.DMA((COPIES,)),
)


class Refs:
    def __init__(self, refs):
        for name, ref in zip(SCRATCH, refs, strict=True):
            setattr(self, name, ref)


def step_kernel(*refs):
    lens_ref = refs[0]
    hbm = refs[1 : 1 + len(INPUTS)]
    out_any, gtok_any, raw_any, stat_any = refs[1 + len(INPUTS) : 5 + len(INPUTS)]
    R = Refs(refs[5 + len(INPUTS) :])
    w4, g4, rc, land = R.w4, R.g4, R.rc, R.land
    me = Place()
    counter = [0]

    def send(src, dst, dev):
        i = counter[0]
        counter[0] += 1
        cp = pltpu.make_async_remote_copy(
            src_ref=src, dst_ref=dst, send_sem=R.ssem.at[i], recv_sem=R.rsem.at[i], device_id=dev, device_id_type=MESH
        )
        cp.start()
        return cp

    other = me.dev(c=1 - me.c)
    w3 = w4.reshape(TILES, D, 128)
    g3 = g4.reshape(TILES, D, 128)

    loads = {}
    for i, (name, src) in enumerate(zip(INPUTS, hbm)):
        cp = pltpu.make_async_copy(src, getattr(R, name), R.lsem.at[i])
        cp.start()
        loads[name] = cp

    barrier = pltpu.get_barrier_semaphore()
    greeted = 0
    for dev in [me.peer(*p)[0] for p in PEERS] + [me.step("x", d) for d in (1, 3)] + [me.far(*p) for p in FARS]:
        pl.semaphore_signal(barrier, inc=1, device_id=dev, device_id_type=MESH)
        greeted += 1
    for name, cp in loads.items():
        if name not in ("tok", "cot"):
            cp.wait()

    vec8 = jnp.concatenate([getattr(R, n)[...].astype(F32) for n in INPUTS[:7]] + [jnp.zeros((1, 6), F32)], axis=0).astype(BF16)
    R.small[...] = (
        nn(R.init[...], one_hot(iota((HEAD, 128), 0) == iota((HEAD, 128), 1)))
        + nn(R.rate[...], one_hot(iota((HEADS, 128), 0) + RATE0 == iota((HEADS, 128), 1)))
        + tn(vec8, one_hot(iota((8, 128), 0) + VEC0 == iota((8, 128), 1)))
    )
    bias_col = tt(one_hot(iota((HEADS, S), 0) + RATE0 == iota((HEADS, S), 1)), R.bias_rate[...])

    srcs = (R.wq, R.wk, R.wv, R.wo, R.wg, R.wu, R.wd, R.small)
    pkf, pk, rv, rv2, stf = R.pkf, R.pk, R.rv, R.rv2, R.stf
    pkf[0] = jnp.zeros((PROWS, 128), F32)
    for h in range(2):
        for xl in range(2):
            for y in range(4):
                i = 0
                for w in OUT_WAVES:
                    for n, t in enumerate(w.mine(h, xl, y)):
                        where = tile_source(w, h, t)
                        if where is not None and (y == 0 or n >= w.nx + w.nz):
                            a, col = where
                            pkf[0, pl.ds(6 * i, 6), :] = srcs[a][:, 128 * col : 128 * col + 128].astype(F32)
                        i += 1
                pk[h * 8 + xl * 4 + y] = pkf[0].astype(BF16)
    pl.semaphore_wait(barrier, greeted)
    firsts = []
    for p in PEERS:
        dev, slot = me.peer(*p)
        firsts.append(send(pk.at[slot], rv.at[me.s], dev))
    rv[pl.ds(me.s, 1)] = pk[pl.ds(me.s, 1)]

    ones = jnp.where(iota((256, 256), 0) // HEAD == iota((256, 256), 1) // HEAD, 1.0 / HEAD, 0.0).astype(BF16)
    rowtok = iota((S, 1), 0)
    mask_r, seg_r = layout_rows(lens_ref, rowtok)
    lane = iota((1, 512), 1)
    ltok = lane // 64 * 16 + lane % 16
    _, seg_l = layout_rows(lens_ref, ltok)
    loads["tok"].wait()
    loads["cot"].wait()
    R.mcot[pl.ds(me.c, 1)] = (R.cot[...].astype(F32) * mask_r).astype(BF16)[None]
    mc_copy = send(R.mcot.at[me.c], R.mcot.at[me.c], other)

    for cp in firsts:
        cp.wait_recv()
    for s in range(16):
        pkf[s] = rv[s].astype(F32)

    def unpack(w, i0):
        for i, t in enumerate(w.mine(me.c, me.xl, me.y)):
            for s in range(16):
                stf[pl.ds(6 * s, 6), :] = pkf[s, pl.ds(6 * (i0 + i), 6), :]
            w4[t, me.z, me.xh] = stf[...].astype(BF16)

    def gather(w, color, forward=()):
        sent = []
        for n, (axis, rect) in enumerate(w.chain(color, me)):
            at = me.coord(axis)
            mine, lo, hi = rect(at), rect((at + 3) % 4), rect((at + 1) % 4)
            now = [send(view(w4, mine), view(w4, mine), me.step(axis, d)) for d in ((1, 3) if n in forward else (1, 3, 2))]
            sent += now
            yield
            for cp in now:
                cp.wait_recv()
            if n in forward:
                now = [
                    send(view(w4, lo, 0), view(w4, lo, 0), me.step(axis, 1)),
                    send(view(w4, hi, 1), view(w4, hi, 1), me.step(axis, 3)),
                ]
                sent += now
                yield
                for cp in now:
                    cp.wait_recv()
        if not w.split:
            off, cnt = w.span(color)
            rect = (w.start(me.c) + off, cnt, ALL, ALL)
            a = send(view(w4, rect), view(w4, rect), other)
            sent.append(a)
            yield
            a.wait_recv()
        for cp in sent:
            cp.wait_send()

    def go(*chains):
        for ch in chains:
            next(ch, None)

    def finish(*chains):
        live = list(chains)
        while live:
            for ch in list(live):
                try:
                    next(ch)
                except StopIteration:
                    live.remove(ch)

    unpack(ONE, 0)
    one_x, one_z = gather(ONE, "x"), gather(ONE, "z")
    three_x = gather(THREE, "x")
    two_x, two_z, two_y = gather(TWO, "x", (1,)), gather(TWO, "z", (1,)), gather(TWO, "y", (2,))
    go(one_x, one_z)
    unpack(THREE, ONE.per)
    unpack(TWO, ONE.per + THREE.per)
    go(two_y, two_x, two_z, three_x)
    go(one_x, one_z)
    go(two_y)
    go(one_x, one_z)
    go(two_x, two_z, two_y, three_x)
    go(one_x, one_z)
    for cp in firsts:
        cp.wait_send()

    def wpair(t):
        return jnp.concatenate([w3[t], w3[t + 1]], axis=1)

    small = w3[TS]
    vsel = one_hot(iota((16, 128), 1) == iota((16, 128), 0) + VEC0)
    vecs = nt(vsel, small)
    norm_gain, init_bias, inner_gain, inner_bias, post_gain, post_bias, mlp_gain = (vecs[i : i + 1] for i in range(7))

    for i in range(4):
        rows = pl.ds(32 * i, 32)
        x = R.tok[rows, :].astype(F32)
        r = lax.rsqrt(jnp.mean(x * x, axis=-1, keepdims=True) + EPS)
        R.nrm[rows, :] = (x * r * norm_gain).astype(BF16)
    normed = R.nrm[...]
    for g in range(GROUPS):
        R.q[:, lanes(g)] = nn(normed, wpair(TQ + 2 * g))
        R.k[:, lanes(g)] = nn(normed, wpair(TK + 2 * g))
        R.v[:, lanes(g)] = nn(normed, wpair(TV + 2 * g))
    sig_t = jax.nn.sigmoid(tt(small, normed) + bias_col)
    rate_t = sig_t * (1.0 / HEAD)
    srow = iota((S, S), 0)
    is_rate = (srow >= RATE0) & (srow < RATE0 + HEADS)
    mask_tok, _ = layout_rows(lens_ref, iota((1, S), 1))
    live = jnp.where(is_rate, rate_t * mask_tok, 0.0)
    rate_sum = jnp.sum(live)
    rate_max = jnp.max(live)
    count = jnp.sum(mask_tok) * HEADS

    tsel = one_hot(iota((S, 512), 0) == ltok)
    rt_hi, rt_lo = split2(rate_t)
    rate_x = nn(rt_hi, tsel) + nn(rt_lo, tsel)
    lane_head = lane // 16 % 4
    jrow = iota((S, 512), 0)
    rate_lane = []
    for g in range(GROUPS):
        here = jrow == RATE0 + 4 * g + lane_head
        rate_lane.append(jnp.sum(jnp.where(here, rate_x, 0.0), axis=0, keepdims=True))
        sel = one_hot(here)
        R.rr[g] = tn(rt_hi, sel) + tn(rt_lo, sel)

    same = seg_r == seg_l
    rmb, rin = rowtok // 16, rowtok % 16
    lmb, lin = lane // 64, lane % 16

    def before():
        return jnp.where(same & (rmb > lmb), 1.0 / MINI, 0.0)

    def after():
        return jnp.where(same & (rmb < lmb), 1.0 / MINI, 0.0)

    def k2():
        return before() + jnp.where((rmb == lmb) & (lin <= rin), 1.0 / (rin + 1).astype(F32), 0.0)

    def k2t():
        return after() + jnp.where((rmb == lmb) & (rin <= lin), 1.0 / (lin + 1).astype(F32), 0.0)

    rep = one_hot(iota((S, 256), 0) == iota((S, 256), 1) % HEAD)
    b0c = init_bias - jnp.concatenate([nn(init_bias[:, 256 * g : 256 * g + 256].astype(BF16), ones) for g in range(GROUPS)], axis=1)
    diag = iota((256, 256), 0) // HEAD == iota((256, 256), 1) // HEAD
    gain2 = inner_gain * inner_gain

    def w0(g):
        wide = nn(w3[TS, 256 * g : 256 * g + 256, :], rep)
        wide = wide - jnp.mean(wide, axis=-1, keepdims=True)
        return split2(jnp.where(diag, wide, 0.0))

    R.u[...] = inner_gain * (inner_bias - R.v[...] + R.k[...])
    for g in range(GROUPS):
        gl = slice(256 * g, 256 * g + 256)
        kb, kl = split2(R.k[:, lanes(g)])
        qb, ql = split2(R.q[:, lanes(g)])
        for m in range(8):
            rows, here = pl.ds(64 * m, 64), slice(16 * m, 16 * m + 16)
            R.kbd[g, rows, :] = block_rows(kb[here])
            R.dbd[g, rows, :] = block_rows(kl[here])
            R.qbd[g, rows, :] = block_rows(qb[here])
        sc = nt(jnp.concatenate([kb, qb, ql], axis=0), R.kbd[g])
        sk = sc[:S] + 1.0
        R.skk[g] = sk
        R.sqk[g] = sc[S : 2 * S] + sc[2 * S :] + nt(qb, R.dbd[g]) + 1.0
        R.pm[g] = (sk * before() * rate_lane[g]).astype(BF16)
        R.pmt[g] = (sk * after() * R.rr[g]).astype(BF16)
        wh, wl = w0(g)
        zz = nn(jnp.concatenate([kb, qb, kl, ql], axis=0), wh)
        zl = nn(jnp.concatenate([kb, qb], axis=0), wl)
        R.zc[:, lanes(g)] = zz[:S] + zz[2 * S : 3 * S] + zl[:S] + b0c[:, gl]
        R.zq[:, lanes(g)] = zz[S : 2 * S] + zz[3 * S :] + zl[S:] + b0c[:, gl]

    def by_group(fn):
        return jnp.concatenate([fn(g, slice(256 * g, 256 * g + 256)) for g in range(GROUPS)], axis=1)

    def seg_mean(x):
        xb = x.astype(BF16)
        return by_group(lambda g, gl: nn(xb[:, gl], ones))

    def seg_mean2(x):
        n = x.shape[0]
        both = jnp.concatenate(split2(x), axis=0)
        r = by_group(lambda g, gl: nn(both[:, gl], ones))
        return r[:n] + r[n:]

    for m in range(8):
        rows = pl.ds(16 * m, 16)
        z = R.zc[rows, :]
        if m > 0:
            h = (m - 1) // 2 * 128
            if h > 0:
                z = z - by_group(lambda g, gl: nn(R.pm[g, rows, 0:h], R.gbd[g, 0:h, :]))
            z = z - by_group(lambda g, gl: nn(R.pm[g, rows, h : 64 * m], R.gbd[g, h : 64 * m, :]))
        uu = R.u[rows, :]
        gz = gain2 * z
        red = seg_mean2(jnp.concatenate([z * z, gz, gz * z, uu * z, uu], axis=0))
        var, r_gz, r_gzz, r_uz, r_u = (red[16 * i : 16 * i + 16] for i in range(5))
        s = lax.rsqrt(var + EPS)
        mg = s * r_gz
        mgg = s * s * r_gzz
        c = mgg + s * r_uz
        zh = z * s
        e = gain2 * zh + uu
        y = e - (mg + r_u) - zh * c
        gh, glow = split2(mask_r[16 * m : 16 * m + 16] * s * y)
        for g in range(GROUPS):
            R.gbd[g, pl.ds(64 * m, 64), :] = block_rows(gh[:, 256 * g : 256 * g + 256])
        R.gh[rows, :] = gh
        R.gl[rows, :] = glow
        R.zc[rows, :] = zh
        R.s1[rows, :] = s
        R.c1[rows, :] = c
        R.e1[rows, :] = e
        R.y1[rows, :] = y
        R.n1[rows, :] = mg
        R.n2[rows, :] = mgg
        if m == 3:
            go(two_x, two_z)
    for g in range(GROUPS):
        gl = slice(256 * g, 256 * g + 256)
        for m in range(8):
            R.dbd[g, pl.ds(64 * m, 64), :] = block_rows(R.gl[16 * m : 16 * m + 16, gl])
        ah, al = split2(R.sqk[g] * (k2() * rate_lane[g]))
        za = nn(jnp.concatenate([ah, al], axis=0), R.gbd[g])
        zb = R.zq[:, lanes(g)] - (za[:S] + za[S:] + nn(ah, R.dbd[g]))
        both = jnp.concatenate(split2(zb * zb), axis=0)
        var = nn(both, ones)
        s2 = lax.rsqrt(var[:S] + var[S:] + EPS)
        zh2 = zb * s2
        R.zq[:, lanes(g)] = zh2
        R.s2[:, lanes(g)] = s2
        R.mix[:, lanes(g)] = R.q[:, lanes(g)] + zh2 * inner_gain[:, gl] + inner_bias[:, gl]

    for i in range(4):
        rows = pl.ds(32 * i, 32)
        x = R.mix[rows, :]
        x = x - jnp.mean(x, axis=-1, keepdims=True)
        p_ = lax.rsqrt(jnp.mean(x * x, axis=-1, keepdims=True) + EPS)
        phat = x * p_
        R.mix[rows, :] = phat
        R.pscale[rows, :] = jnp.broadcast_to(p_, (32, 128))
        R.post[rows, :] = (phat * post_gain + post_bias).astype(BF16)
    pb = R.post[...]
    mc_copy.wait_recv()
    R.xt[1] = R.mcot[...].reshape(2 * S, D).T
    go(two_y)
    finish(three_x, one_x, one_z)

    def out_pair(g):
        return jnp.concatenate([w3[tile_out(2 * g)], w3[tile_out(2 * g + 1)]], axis=1)

    for g in range(GROUPS):
        R.hid[:, lanes(g)] = R.tok[:, lanes(g)].astype(F32) + nn(pb, out_pair(g))
    for i in range(4):
        rows = pl.ds(32 * i, 32)
        x = R.hid[rows, :]
        r = lax.rsqrt(jnp.mean(x * x, axis=-1, keepdims=True) + EPS)
        R.nrm2[pl.ds(me.c, 1), rows, :] = (x * r * mlp_gain).astype(BF16)[None]
    n2_copy = send(R.nrm2.at[me.c], R.nrm2.at[me.c], other)
    for t in PADS:
        g3[t] = jnp.zeros((D, 128), BF16)
    n2_copy.wait_recv()
    R.xt[0] = R.nrm2[...].reshape(2 * S, D).T
    finish(two_x, two_z, two_y)

    used = [0]

    def reduce(w, color, forward=()):
        off, cnt = w.span(color)
        sent = []
        if not w.split:
            landed = (0 if w is LAST else LAST.half) + off
            own = w.start(me.c) + off
            a = send(g4.at[pl.ds(w.start(1 - me.c) + off, cnt)], rc.at[pl.ds(landed, cnt)], other)
            sent.append(a)
            yield
            a.wait_recv()

            def add_tile(t, carry):
                for z in range(4):
                    for xh in range(2):
                        g4[own + t, z, xh] = (g4[own + t, z, xh].astype(F32) + rc[landed + t, z, xh].astype(F32)).astype(BF16)
                return carry

            lax.fori_loop(0, cnt, add_tile, 0)
        for n, (axis, rect) in enumerate(reversed(w.chain(color, me))):
            at = me.coord(axis)
            size, place = blocks(rect(at))
            base = used[0]
            used[0] += 3 * size
            _, nt_, z, xh = rect(at)
            lead = (nt_,) + ((4,) if z is ALL else ()) + ((2,) if xh is ALL else ())

            def slot(i, half=None, base=base, size=size, lead=lead):
                rows = ALL if half is None else pl.ds(48 * half, 48)
                return land.at[pl.ds(base + i * size, size)].reshape(*lead, 96, 128).at[(ALL,) * len(lead) + (rows,)]

            right, left, far = rect((at + 1) % 4), rect((at + 3) % 4), rect((at + 2) % 4)
            if n in forward:
                now = [
                    send(view(g4, far, 0), slot(2, 0), me.step(axis, 1)),
                    send(view(g4, far, 1), slot(2, 1), me.step(axis, 3)),
                ]
                sent += now
                yield
                for cp in now:
                    cp.wait_recv()
                right_at, left_at = blocks(right)[1], blocks(left)[1]

                def add_far(i, carry, base=base, size=size, right_at=right_at, left_at=left_at):
                    for half, where in ((0, right_at), (1, left_at)):
                        p = where(i) + (pl.ds(48 * half, 48),)
                        g4[p] = (g4[p].astype(F32) + land[base + 2 * size + i, pl.ds(48 * half, 48)].astype(F32)).astype(BF16)
                    return carry

                lax.fori_loop(0, size, add_far, 0)
                now = [send(view(g4, right), slot(0), me.step(axis, 1)), send(view(g4, left), slot(1), me.step(axis, 3))]
            else:
                now = [
                    send(view(g4, right), slot(0), me.step(axis, 1)),
                    send(view(g4, left), slot(1), me.step(axis, 3)),
                    send(view(g4, far), slot(2), me.step(axis, 2)),
                ]
            sent += now
            yield
            for cp in now:
                cp.wait_recv()
            terms = len(now)

            def add_mine(i, carry, base=base, size=size, place=place, terms=terms):
                p = place(i)
                total = g4[p].astype(F32)
                for k_ in range(terms):
                    total += land[base + k_ * size + i].astype(F32)
                g4[p] = total.astype(BF16)
                return carry

            lax.fori_loop(0, size, add_mine, 0)
        for cp in sent:
            cp.wait_send()

    back_y, back_z, back_x = reduce(FIRST, "y", (0,)), reduce(FIRST, "z", (0,)), reduce(FIRST, "x", (0,))

    x2, mc = R.nrm2[...].reshape(2 * S, D), R.mcot[...].reshape(2 * S, D)
    for j in reversed(range(4)):
        wg, wu, wd = (wpair(tile_mlp(j, kind)) for kind in range(3))
        gate, up, ac = nn(x2, wg), nn(x2, wu), nn(mc, wd)
        sg = jax.nn.sigmoid(gate)
        silu = gate * sg
        a = (silu * up).astype(BF16)
        gc = (ac * up * (sg * (1.0 + gate * (1.0 - sg)))).astype(BF16)
        uc = (ac * silu).astype(BF16)
        o_part = nt(a, wd).reshape(2, S, D)
        t_part = (nt(gc, wg) + nt(uc, wu)).reshape(2, S, D)
        if j == 3:
            R.o2[...] = o_part
            R.t2[...] = t_part
        else:
            R.o2[...] += o_part
            R.t2[...] += t_part
        for h in range(2):
            sl = slice(128 * h, 128 * h + 128)
            g3[tile_mlp(j, 0) + h] = nn(R.xt[0], gc[:, sl]).astype(BF16)
            g3[tile_mlp(j, 1) + h] = nn(R.xt[0], uc[:, sl]).astype(BF16)
            g3[tile_mlp(j, 2) + h] = nn(R.xt[1], a[:, sl]).astype(BF16)
        if j == 2:
            go(back_y)
        if j == 1:
            go(back_z)
    t_copy = send(R.t2.at[1 - me.c], R.t_in, other)
    go(back_x)
    o_copy = send(R.o2.at[1 - me.c], R.o_in, other)

    t_copy.wait_recv()
    g_mlp_gain = jnp.zeros((1, D), F32)
    for i in range(4):
        rows = pl.ds(32 * i, 32)
        mr = mask_r[32 * i : 32 * i + 32]
        x = R.hid[rows, :]
        r = lax.rsqrt(jnp.mean(x * x, axis=-1, keepdims=True) + EPS)
        u = x * r
        t = R.t2[pl.ds(me.c, 1), rows, :][0] + R.t_in[rows, :]
        g_mlp_gain += jnp.sum(t * u, axis=0, keepdims=True)
        c = t * mlp_gain
        h = mr * R.cot[rows, :].astype(F32) + r * (c - u * jnp.mean(c * u, axis=-1, keepdims=True))
        R.hcot[rows, :] = h
        R.bcot[rows, :] = h.astype(BF16)

    bc = R.bcot[...]
    pt_ = pb.T
    for c_ in range(6):
        g3[tile_out(c_)] = nn(pt_, bc[:, 128 * c_ : 128 * c_ + 128]).astype(BF16)
    go(back_y, back_z)
    acc = nt(bc[:, 0:256], out_pair(0))
    for g in range(1, GROUPS):
        acc += nt(bc[:, 256 * g : 256 * g + 256], out_pair(g))
    R.tcot[...] = acc
    go(back_x)
    o_copy.wait_recv()
    for i in range(4):
        rows = pl.ds(32 * i, 32)
        o = R.hid[rows, :] + R.o2[pl.ds(me.c, 1), rows, :][0] + R.o_in[rows, :]
        R.out[rows, :] = (mask_r[32 * i : 32 * i + 32] * o).astype(BF16)
    out_copy = pltpu.make_async_copy(R.out, out_any, R.lsem.at[0])
    out_copy.start()
    g_post_gain = jnp.zeros((1, D), F32)
    g_post_bias = jnp.zeros((1, D), F32)
    for i in range(4):
        rows = pl.ds(32 * i, 32)
        pc = R.tcot[rows, :]
        phat = R.mix[rows, :]
        g_post_gain += jnp.sum(pc * phat, axis=0, keepdims=True)
        g_post_bias += jnp.sum(pc, axis=0, keepdims=True)
        e = pc * post_gain
        R.tcot[rows, :] = R.pscale[rows, 0:1] * (
            e - jnp.mean(e, axis=-1, keepdims=True) - phat * jnp.mean(e * phat, axis=-1, keepdims=True)
        )

    do, zh2 = R.tcot[...], R.zq[...]
    g_inner_gain = jnp.sum(do * zh2, axis=0, keepdims=True)
    g_inner_bias = jnp.sum(do, axis=0, keepdims=True)
    dz = do * inner_gain
    dzb = R.s2[...] * (dz - zh2 * seg_mean(dz * zh2))
    gb_rows = jnp.sum(dzb, axis=0, keepdims=True)
    R.dzb[...] = dzb.astype(BF16)
    R.zbd[...] = jnp.zeros(R.zbd.shape, BF16)
    for g in range(GROUPS):
        db = R.dzb[:, lanes(g)]
        for m in range(8):
            R.dbd[g, pl.ds(64 * m, 64), :] = block_rows(db[16 * m : 16 * m + 16])
        kb = R.k[:, lanes(g)].astype(BF16)
        at = (nt(kb, R.qbd[g]) + 1.0) * (k2t() * R.rr[g])
        R.dgr[:, lanes(g)] = -nn(at.astype(BF16), R.dbd[g])

    for m in reversed(range(8)):
        rows = pl.ds(16 * m, 16)
        dg = R.dgr[rows, :]
        if m < 7:
            h = (m + 1) // 2 * 128
            if h + 128 < 512:
                dg = dg - by_group(lambda g, gl: nn(R.pmt[g, rows, h + 128 : 512], R.zbd[g, h + 128 : 512, :]))
            dg = dg - by_group(lambda g, gl: nn(R.pmt[g, rows, h : h + 128], R.zbd[g, h : h + 128, :]))
        hh = mask_r[16 * m : 16 * m + 16] * dg
        s, c, zh, e, y = R.s1[rows, :], R.c1[rows, :], R.zc[rows, :], R.e1[rows, :], R.y1[rows, :]
        zhh = zh * hh
        red = seg_mean(jnp.concatenate([hh, zhh, gain2 * zhh, y * hh], axis=0))
        m0, m1, m2, m3 = (red[16 * i : 16 * i + 16] for i in range(4))
        de = s * (hh - m0 - zh * m1)
        dzh = gain2 * de - s * (c * hh + e * m1)
        t = m2 - 2.0 * c * m1 - m0 * R.n1[rows, :] - m1 * R.n2[rows, :]
        dzc = s * (dzh - zh * (s * (m3 + t)))
        db = dzc.astype(BF16)
        for g in range(GROUPS):
            R.zbd[g, pl.ds(64 * m, 64), :] = block_rows(db[:, 256 * g : 256 * g + 256])
        R.dzc[rows, :] = db
        R.dgr[rows, :] = de
        R.dzf[rows, :] = dzc

    de = R.dgr[...]
    g_inner_gain += jnp.sum(de * (inner_bias - R.v[...] + R.k[...] + 2.0 * inner_gain * R.zc[...]), axis=0, keepdims=True)
    gde_all = inner_gain * de
    g_inner_bias += jnp.sum(gde_all, axis=0, keepdims=True)
    bsum = gb_rows + jnp.sum(R.dzf[...], axis=0, keepdims=True)
    g_init_bias = bsum - seg_mean2(jnp.broadcast_to(bsum, (16, D)))[0:1]
    x1t = R.nrm[...].T
    dv_all = (-gde_all).astype(BF16)
    for c_ in range(6):
        g3[TV + c_] = nn(x1t, dv_all[:, 128 * c_ : 128 * c_ + 128]).astype(BF16)
    mid_x, mid_z = reduce(MID, "x"), reduce(MID, "z")
    go(mid_x, mid_z)
    logit_acc = jnp.zeros((S, S), F32)
    wgrad_small = []
    for g in range(GROUPS):
        gl = slice(256 * g, 256 * g + 256)
        gde = inner_gain[:, gl] * R.dgr[:, lanes(g)]
        dzb_b, dzc_b = R.dzb[:, lanes(g)], R.dzc[:, lanes(g)]
        kb = R.k[:, lanes(g)].astype(BF16)
        qb = R.q[:, lanes(g)].astype(BF16)
        gb = R.gh[:, lanes(g)]
        rl, rr = rate_lane[g], R.rr[g]
        dd = nt(jnp.concatenate([dzb_b, dzc_b], axis=0), R.gbd[g])
        dr = -dd[:S] * k2()
        dp = -dd[S:] * before()
        drate = jnp.sum(dr * R.sqk[g] + dp * R.skk[g], axis=0, keepdims=True)
        dat = -nt(gb, R.dbd[g])
        dpt = -nt(gb, R.zbd[g])
        low = jnp.concatenate([(dr * rl).astype(BF16), (dp * rl + dpt * (after() * rr)).astype(BF16)], axis=0)
        dqk = nn(low, R.kbd[g])
        wh, _ = w0(g)
        dqk += nt(jnp.concatenate([dzb_b, dzc_b], axis=0), wh)
        dq = R.tcot[:, lanes(g)] + dqk[:S]
        dk = gde + dqk[S:] + nn((dat * (k2t() * rr)).astype(BF16), R.qbd[g])
        gwide = jnp.where(diag, tn(qb, dzb_b) + tn(kb, dzc_b), 0.0)
        fold = one_hot(iota((256, 128), 0) % HEAD == iota((256, 128), 1))
        gw_hi, gw_lo = split2(gwide)
        gsm = nn(gw_hi, fold) + nn(gw_lo, fold)
        wgrad_small.append(
            gsm - jnp.where(iota((256, 128), 1) < HEAD, jnp.sum(gsm, axis=-1, keepdims=True) * (1.0 / HEAD), 0.0)
        )
        dl = drate * rl * (1.0 - rl * HEAD)
        dlx = jnp.where(jrow == RATE0 + 4 * g + lane_head, dl, 0.0)
        logit_acc += nt(dlx.astype(BF16), tsel)
        dqb, dkb, dvb = dq.astype(BF16), dk.astype(BF16), (-gde).astype(BF16)
        for h in range(2):
            sl = slice(128 * h, 128 * h + 128)
            g3[TQ + 2 * g + h] = nn(x1t, dqb[:, sl]).astype(BF16)
            g3[TK + 2 * g + h] = nn(x1t, dkb[:, sl]).astype(BF16)
        part = nt(dqb, wpair(TQ + 2 * g)) + nt(dkb, wpair(TK + 2 * g)) + nt(dvb, wpair(TV + 2 * g))
        if g == 0:
            R.ot[...] = part
        else:
            R.ot[...] += part

    last_x, last_z = reduce(LAST, "x"), reduce(LAST, "z")
    go(last_x, mid_x, mid_z, back_y)
    logit_b = logit_acc.astype(BF16)
    oc_all = R.ot[...] + tt(logit_b, small)
    R.ot[...] = oc_all
    g_bias = jnp.sum(logit_acc, axis=1, keepdims=True)
    g_rate = nt(x1t, logit_b)
    g_norm_gain = jnp.zeros((1, D), F32)
    for i in range(4):
        rows = pl.ds(32 * i, 32)
        x = R.tok[rows, :].astype(F32)
        r = lax.rsqrt(jnp.mean(x * x, axis=-1, keepdims=True) + EPS)
        g_norm_gain += jnp.sum(R.ot[rows, :] * (x * r), axis=0, keepdims=True)

    vec_rows = jnp.concatenate(
        [g_norm_gain, g_init_bias, g_inner_gain, g_inner_bias, g_post_gain, g_post_bias, g_mlp_gain, jnp.zeros((9, D), F32)], axis=0
    ).astype(BF16)
    g3[TS] = (jnp.concatenate(wgrad_small, axis=0) + g_rate + tn(vec_rows, vsel)).astype(BF16)
    go(last_z)

    bias_row = jnp.sum(jnp.where(iota((S, S), 0) == iota((S, S), 1), g_bias, 0.0), axis=0, keepdims=True)
    r8 = iota((8, 128), 0)
    R.stat[...] = jnp.where(
        r8 == 0, rate_sum, jnp.where(r8 == 1, count, jnp.where(r8 == 2, rate_max, jnp.where(r8 == 3, bias_row, 0.0)))
    )
    stats = [send(R.stat, R.sa.at[me.s], me.peer(*p)[0]) for p in PEERS]
    R.sa[pl.ds(me.s, 1)] = R.stat[...][None]
    for i in range(4):
        rows = pl.ds(32 * i, 32)
        x = R.tok[rows, :].astype(F32)
        r = lax.rsqrt(jnp.mean(x * x, axis=-1, keepdims=True) + EPS)
        w = x * r
        f = R.ot[rows, :] * norm_gain
        R.gtok[rows, :] = (R.hcot[rows, :] + r * (f - w * jnp.mean(f * w, axis=-1, keepdims=True))).astype(BF16)
    gtok_copy = pltpu.make_async_copy(R.gtok, gtok_any, R.lsem.at[1])
    gtok_copy.start()

    go(last_x, back_z, back_x, last_z)

    def combine(buf, n):
        total, peak = buf[0], buf[0]
        for s in range(1, n):
            total, peak = total + buf[s], jnp.maximum(peak, buf[s])
        return jnp.where(r8 == 2, peak, total)

    for cp in stats:
        cp.wait_recv()
    R.sb[pl.ds(me.zx, 1)] = combine(R.sa, 16)[None]
    stats2 = [send(R.sb.at[me.zx], R.sb.at[me.zx], me.far(*p)) for p in FARS]
    finish(mid_x, mid_z, back_y, last_x, last_z, back_z, back_x)

    i = 0
    for w in BACK_WAVES:
        for t in w.mine(me.c, me.xl, me.y):
            stf[...] = g4[t, me.z, me.xh].astype(F32)
            for s in range(16):
                pkf[s, pl.ds(6 * i, 6), :] = stf[pl.ds(6 * s, 6), :]
            i += 1
    for s in range(16):
        pk[s] = pkf[s].astype(BF16)
    last = []
    for p in PEERS:
        dev, slot = me.peer(*p)
        last.append(send(pk.at[slot], rv2.at[me.s], dev))
    rv2[pl.ds(me.s, 1)] = pk[pl.ds(me.s, 1)]
    for cp in stats2:
        cp.wait_recv()
    R.stat_sum[...] = combine(R.sb, 8)
    stat_copy = pltpu.make_async_copy(R.stat_sum, stat_any, R.lsem.at[2])
    stat_copy.start()
    for cp in last:
        cp.wait_recv()
    raw_copy = pltpu.make_async_copy(rv2, raw_any, R.lsem.at[3])
    raw_copy.start()
    for cp in [mc_copy, n2_copy, t_copy, o_copy] + stats + stats2 + last:
        cp.wait_send()
    for cp in (out_copy, gtok_copy, stat_copy, raw_copy):
        cp.wait()


def step(lens, *arrays):
    anym = pl.BlockSpec(memory_space=pl.ANY)
    sd = jax.ShapeDtypeStruct
    return pl.pallas_call(
        step_kernel,
        out_shape=(sd((S, D), BF16), sd((S, D), BF16), sd((16, PROWS, 128), BF16), sd((8, 128), F32)),
        in_specs=[pl.BlockSpec(memory_space=pltpu.SMEM)] + [anym] * len(INPUTS),
        out_specs=(anym,) * 4,
        scratch_shapes=list(SCRATCH.values()),
        compiler_params=pltpu.CompilerParams(collective_id=0, has_side_effects=True, vmem_limit_bytes=60 * 2**20),
        name="step",
    )(lens, *arrays)


def finish_kernel(raw, stat, out_in, gtok_in, *outs):
    (out, gtok, g_norm, gq, gk, gv, g_rate, g_brate, g_init, g_ib, g_ig, g_ibias, g_pg, g_pb, go, g_mg, gg, gu, gd,
     r_mean, r_max, pkf) = outs
    out[...] = out_in[...]
    gtok[...] = gtok_in[...]
    mats = (gq, gk, gv, go, gg, gu, gd)
    for s in range(16):
        pkf[s] = raw[s].astype(F32)
    for h in range(2):
        for xl in range(2):
            i = 0
            for w in BACK_WAVES:
                for n in range(w.per):
                    for y in range(4 if n >= w.nx + w.nz else 1):
                        where = tile_source(w, h, w.mine(h, xl, y)[n])
                        if where is None:
                            continue
                        if n < w.nx + w.nz:
                            x = [pkf[h * 8 + xl * 4 + y_, pl.ds(6 * i, 6), :] for y_ in range(4)]
                            val = (x[0] + x[1]) + (x[2] + x[3])
                        else:
                            val = pkf[h * 8 + xl * 4 + y, pl.ds(6 * i, 6), :]
                        a, col = where
                        if a < A_S:
                            mats[a][:, 128 * col : 128 * col + 128] = val
                        else:
                            g_init[...] = val[:, :HEAD]
                            g_rate[...] = val[:, RATE0 : RATE0 + HEADS]
                            vt = val.T
                            for n_, ref in enumerate((g_norm, g_ib, g_ig, g_ibias, g_pg, g_pb, g_mg)):
                                ref[...] = vt[VEC0 + n_ : VEC0 + n_ + 1, :]
                    i += 1
    st = stat[...]
    g_brate[...] = st[3:4, RATE0 : RATE0 + HEADS]
    r_mean[...] = st[0:1, 0:1] / st[1:2, 0:1]
    r_max[...] = st[2:3, 0:1]


def finish_call(raw, stat, out, gtok):
    vm = pl.BlockSpec(memory_space=pltpu.VMEM)
    sd = jax.ShapeDtypeStruct
    row = sd((1, 6), F32)
    m768, m2048 = sd((6, 768), F32), sd((6, FF), F32)
    shapes = (
        sd((S, D), BF16), sd((S, D), BF16), row, m768, m768, m768, sd((6, HEADS), F32), sd((1, HEADS), F32),
        sd((6, HEAD), F32), row, row, row, row, row, m768, row, m2048, m2048, m2048, sd((1, 1), F32), sd((1, 1), F32),
    )
    return pl.pallas_call(
        finish_kernel, out_shape=shapes, in_specs=[vm] * 4, out_specs=(vm,) * 21,
        scratch_shapes=[pltpu.VMEM((16, PROWS, 128), F32)], name="finish",
    )(raw, stat, out, gtok)


def per_device(
    tokens, cotangent, seq_lengths, norm_gain, weight_query, weight_key, weight_value, weight_rate, bias_rate,
    init_weight, init_bias, inner_gain, inner_bias, post_gain, post_bias, weight_out, mlp_gain, weight_gate, weight_up,
    weight_down,
):
    rows = (norm_gain, init_bias, inner_gain, inner_bias, post_gain, post_bias, mlp_gain)
    out, gtok, raw, stat = step(
        seq_lengths, *[r.reshape(1, -1) for r in rows + (bias_rate,)], tokens, cotangent, weight_query, weight_key, weight_value, weight_out, weight_gate, weight_up,
        weight_down, init_weight, weight_rate,
    )
    res = list(finish_call(raw, stat, out, gtok))
    for i in (2, 9, 10, 11, 12, 13, 15):
        res[i] = res[i].reshape(6)
    res[7] = res[7].reshape(HEADS)
    res[19], res[20] = res[19].reshape(()), res[20].reshape(())
    return tuple(res)


def solution(mesh):
    both = ("dp", "sub")
    mat, vec, rep = P(both, None), P(both), P()
    return jax.shard_map(
        per_device,
        mesh=mesh,
        in_specs=(mat, mat, mat, vec, mat, mat, mat, mat, rep, mat, vec, vec, vec, vec, vec, mat, vec, mat, mat, mat),
        out_specs=(mat, mat, vec, mat, mat, mat, mat, rep, mat, vec, vec, vec, vec, vec, mat, vec, mat, mat, mat, rep, rep),
        check_vma=False,
    )
```

time: 3890 us -> 129 us (0.03)
  blocking collectives: 1260 us -> 0 us
  waiting for transfers between devices: 1230 us -> 0 us
  starting transfers between devices: 618 us -> 0 us
  local copies, waits for them, and re-layouts: 328 us -> 0 us
  matrix products: 217 us -> 0 us
  other arithmetic: 169 us -> 0 us
  Pallas kernels: 0 us -> 128 us
    all_gather x7 -> x0, waiting for transfers between devices: 1230 us -> none  [the longest x1 303 us: per_device(): lax.all_gather(weight_up, ('dp', 'sub'), axis=0, tiled=True)]
    unnamed x225 -> x0, starting transfers between devices: 617 us -> none
    all_gather x2 -> x0, blocking collectives: 609 us -> none  [the longest x1 312 us: per_device(): lax.all_gather(init_weight, ('dp', 'sub'), axis=0, tiled=True)]
    unnamed x3 -> x0, blocking collectives: 583 us -> none
    unnamed x484 -> x0, local copies, waits for them, and re-layouts: 241 us -> none
    dot_general x144 -> x0, matrix products: 217 us -> none  [the longest x24 44.4 us: advance(): jnp.einsum('svf,sfl->svl', key_minibatch, current_weight, precision=preci...]
    pallas_call x0 -> x2, Pallas kernels: none -> 128 us  [the longest x1 126 us: step(): pl.pallas_call(step_kernel, out_shape=(sd((S, D), BF16), sd((S, D), BF16)...]
    dynamic_update_slice x64 -> x0, other arithmetic: 75 us -> none  [inner_mixer(): lax.scan(advance, initial, (heads_first(queries), heads_first(key_rows),...]
  transfers between devices with their start and end apart: 232 -> 0, of which waited for: 6 -> 0; matrix products, arithmetic and copies ran while one was open for 11% -> 0% of each run, Pallas kernels for 0% -> 0%
where the time goes in v1:
time: 129 us
  Pallas kernels  128 us (99%)
    pallas_call x1, Pallas kernels, step(): pl.pallas_call(step_kernel, out_shape=(sd((S, D), BF16), sd((S, D), BF16)...  126 us

profile of v1, /device:TPU:1, one launch (start us, length us, event | category | flops | bytes accessed | tf_op | source)
XLA Modules:
  0.0 128.6 jit_solution(6807931054761051912)
XLA Ops:
  0.7 125.7 %step.1 = (bf16[128,768]{1,0:T(8,128)(2,1)}, bf16[128,768]{1,0:T(8,128)(2,1)}, bf16[16,96,128]{2,1,0:T(8,128)(2,1)}, f32[8,128]{1,0:T(8,128)}) custom-call(s32[1,4]{1,0:T(1,128)} %refs_0_.1, bf16[1,6]{1,0:T(2,128)(2,1)} %bitcast.18, bf16[1,6]{1,0:T(2,128)(2,1)} %bitcast.19, bf16[1,6]{1,0:T(2,128)(2,1)} %bitcast.20, bf16[1,6]{1,0:T(2,128)(2,1)} %bitcast.21, ...), custom_call_target="tpu_custom_call" | custom-call | tf_op jit(solution)/shard_map/step/pallas_call | solution.py:930
  126.3 2.1 %finish.1 = (bf16[128,768]{1,0:T(8,128)(2,1)}, bf16[128,768]{1,0:T(8,128)(2,1)}, f32[1,6]{1,0:T(1,128)}, f32[6,768]{1,0:T(8,128)}, f32[6,768]{1,0:T(8,128)}, /*i...) custom-call(bf16[16,96,128]{2,1,0:T(8,128)(2,1)} %get-tuple-element., ...), custom_call_target="tpu_custom_call" | custom-call | tf_op jit(solution)/shard_map/finish/pallas_call | solution.py:988

commit v2 on v1

--- a/solution.py
+++ b/solution.py
@@ -75,9 +75,9 @@
         return [k for k in order if {"x": self.nx, "z": self.nz, "y": self.ny}[k]]
 
 
-ONE, THREE, TWO = Wave(0, 3, 3, 0), Wave(24, 1, 0, 0), Wave(28, 4, 4, 1, split=True)
+ONE, THREE, TWO = Wave(0, 3, 3, 0), Wave(24, 0, 1, 0), Wave(28, 4, 4, 1, split=True)
 OUT_WAVES = (ONE, THREE, TWO)
-LAST, MID, FIRST = Wave(0, 2, 2, 0), Wave(16, 2, 1, 0), Wave(28, 4, 4, 1, split=True)
+LAST, MID, FIRST = Wave(0, 2, 2, 0), Wave(16, 1, 2, 0), Wave(28, 4, 4, 1, split=True)
 BACK_WAVES = (LAST, MID, FIRST)
 TILES = 52
 PER = max(sum(w.per for w in ws) for ws in (OUT_WAVES, BACK_WAVES))
@@ -224,7 +224,27 @@
 
 
 BACK_SLOTS = back_slots()
-COPIES = sum((len(w.chain(k, Zero)) * 8 + 2) for w in OUT_WAVES + BACK_WAVES for k in w.colors()) + 3 * len(PEERS) + len(FARS) + 8
+
+
+def steps_forward(w, color, back):
+    if w.split:
+        if back:
+            return {"x": (0,), "z": (0,), "y": (0, 1)}[color]
+        return {"x": (1,), "z": (1,), "y": (1, 2)}[color]
+    if back:
+        return (0,)
+    return (1,) if w is ONE else ()
+
+
+def copies_of(w, color, back):
+    fwd = steps_forward(w, color, back)
+    return sum(4 if n in fwd else 3 for n in range(len(w.chain(color, Zero)))) + (0 if w.split else 1)
+
+
+OUT_COPIES = sum(copies_of(w, k, False) for w in OUT_WAVES for k in w.colors())
+BACK_COPIES = sum(copies_of(w, k, True) for w in BACK_WAVES for k in w.colors())
+RECV_SEMS = OUT_COPIES + BACK_COPIES + 8
+SEND_SEMS = max(OUT_COPIES, BACK_COPIES) + 8
 
 
 def view(ref, rect, half=None):
@@ -258,7 +278,7 @@
     rr=f32(GROUPS, S, 512), pscale=f32(S, 128), hcot=f32(S, D), bcot=b16(S, D), tcot=f32(S, D), ot=f32(S, D), out=b16(S, D),
     gtok=b16(S, D),
     nrm2=b16(2, S, D), mcot=b16(2, S, D), xt=b16(2, D, 2 * S), t2=f32(2, S, D), o2=f32(2, S, D), t_in=f32(S, D), o_in=f32(S, D),
-    lsem=pltpu.SemaphoreType.DMA((len(INPUTS),)), ssem=pltpu.SemaphoreType.DMA((COPIES,)), rsem=pltpu.SemaphoreType.DMA((COPIES,)),
+    lsem=pltpu.SemaphoreType.DMA((len(INPUTS),)), ssem=pltpu.SemaphoreType.DMA((SEND_SEMS,)), rsem=pltpu.SemaphoreType.DMA((RECV_SEMS,)),
 )
 
 
@@ -275,16 +295,26 @@
     R = Refs(refs[5 + len(INPUTS) :])
     w4, g4, rc, land = R.w4, R.g4, R.rc, R.land
     me = Place()
-    counter = [0]
-
-    def send(src, dst, dev):
-        i = counter[0]
-        counter[0] += 1
-        cp = pltpu.make_async_remote_copy(
-            src_ref=src, dst_ref=dst, send_sem=R.ssem.at[i], recv_sem=R.rsem.at[i], device_id=dev, device_id_type=MESH
+    taken = {"group": 0, "out": 8, "back": 8}
+
+    def copy(src, dst, dev, i, j):
+        return pltpu.make_async_remote_copy(
+            src_ref=src, dst_ref=dst, send_sem=R.ssem.at[i], recv_sem=R.rsem.at[j], device_id=dev, device_id_type=MESH
         )
+
+    def send(src, dst, dev, kind="group"):
+        i = taken[kind]
+        taken[kind] += 1
+        cp = copy(src, dst, dev, i, i + OUT_COPIES if kind == "back" else i)
         cp.start()
         return cp
+
+    def send_all(triples, whole):
+        i = taken["group"]
+        taken["group"] += 1
+        for src, dst, dev in triples:
+            copy(src, dst, dev, i, i).start()
+        return copy(whole, whole, me.dev(), i, i)
 
     other = me.dev(c=1 - me.c)
     w3 = w4.reshape(TILES, D, 128)
@@ -329,10 +359,8 @@
                         i += 1
                 pk[h * 8 + xl * 4 + y] = pkf[0].astype(BF16)
     pl.semaphore_wait(barrier, greeted)
-    firsts = []
-    for p in PEERS:
-        dev, slot = me.peer(*p)
-        firsts.append(send(pk.at[slot], rv.at[me.s], dev))
+    peers = [me.peer(*p) for p in PEERS]
+    firsts = send_all([(pk.at[slot], rv.at[me.s], dev) for dev, slot in peers], rv.at[pl.ds(0, 15)])
     rv[pl.ds(me.s, 1)] = pk[pl.ds(me.s, 1)]
 
     ones = jnp.where(iota((256, 256), 0) // HEAD == iota((256, 256), 1) // HEAD, 1.0 / HEAD, 0.0).astype(BF16)
@@ -346,8 +374,7 @@
     R.mcot[pl.ds(me.c, 1)] = (R.cot[...].astype(F32) * mask_r).astype(BF16)[None]
     mc_copy = send(R.mcot.at[me.c], R.mcot.at[me.c], other)
 
-    for cp in firsts:
-        cp.wait_recv()
+    firsts.wait_recv()
     for s in range(16):
         pkf[s] = rv[s].astype(F32)
 
@@ -357,20 +384,21 @@
                 stf[pl.ds(6 * s, 6), :] = pkf[s, pl.ds(6 * (i0 + i), 6), :]
             w4[t, me.z, me.xh] = stf[...].astype(BF16)
 
-    def gather(w, color, forward=()):
+    def gather(w, color):
+        forward = steps_forward(w, color, False)
         sent = []
         for n, (axis, rect) in enumerate(w.chain(color, me)):
             at = me.coord(axis)
             mine, lo, hi = rect(at), rect((at + 3) % 4), rect((at + 1) % 4)
-            now = [send(view(w4, mine), view(w4, mine), me.step(axis, d)) for d in ((1, 3) if n in forward else (1, 3, 2))]
+            now = [send(view(w4, mine), view(w4, mine), me.step(axis, d), "out") for d in ((1, 3) if n in forward else (1, 3, 2))]
             sent += now
             yield
             for cp in now:
                 cp.wait_recv()
             if n in forward:
                 now = [
-                    send(view(w4, lo, 0), view(w4, lo, 0), me.step(axis, 1)),
-                    send(view(w4, hi, 1), view(w4, hi, 1), me.step(axis, 3)),
+                    send(view(w4, lo, 0), view(w4, lo, 0), me.step(axis, 1), "out"),
+                    send(view(w4, hi, 1), view(w4, hi, 1), me.step(axis, 3), "out"),
                 ]
                 sent += now
                 yield
@@ -379,7 +407,7 @@
         if not w.split:
             off, cnt = w.span(color)
             rect = (w.start(me.c) + off, cnt, ALL, ALL)
-            a = send(view(w4, rect), view(w4, rect), other)
+            a = send(view(w4, rect), view(w4, rect), other, "out")
             sent.append(a)
             yield
             a.wait_recv()
@@ -401,19 +429,20 @@
 
     unpack(ONE, 0)
     one_x, one_z = gather(ONE, "x"), gather(ONE, "z")
-    three_x = gather(THREE, "x")
-    two_x, two_z, two_y = gather(TWO, "x", (1,)), gather(TWO, "z", (1,)), gather(TWO, "y", (2,))
+    three_z = gather(THREE, "z")
+    two_x, two_z, two_y = gather(TWO, "x"), gather(TWO, "z"), gather(TWO, "y")
     go(one_x, one_z)
     unpack(THREE, ONE.per)
     unpack(TWO, ONE.per + THREE.per)
-    go(two_y, two_x, two_z, three_x)
+    go(two_y, two_x, two_z, three_z)
     go(one_x, one_z)
     go(two_y)
     go(one_x, one_z)
-    go(two_x, two_z, two_y, three_x)
+    go(two_y, two_x, two_z)
     go(one_x, one_z)
-    for cp in firsts:
-        cp.wait_send()
+    go(two_y, three_z)
+    go(one_x, one_z)
+    firsts.wait_send()
 
     def wpair(t):
         return jnp.concatenate([w3[t], w3[t + 1]], axis=1)
@@ -577,7 +606,7 @@
     mc_copy.wait_recv()
     R.xt[1] = R.mcot[...].reshape(2 * S, D).T
     go(two_y)
-    finish(three_x, one_x, one_z)
+    finish(three_z, one_x, one_z)
 
     def out_pair(g):
         return jnp.concatenate([w3[tile_out(2 * g)], w3[tile_out(2 * g + 1)]], axis=1)
@@ -598,13 +627,14 @@
 
     used = [0]
 
-    def reduce(w, color, forward=()):
+    def reduce(w, color):
+        forward = steps_forward(w, color, True)
         off, cnt = w.span(color)
         sent = []
         if not w.split:
             landed = (0 if w is LAST else LAST.half) + off
             own = w.start(me.c) + off
-            a = send(g4.at[pl.ds(w.start(1 - me.c) + off, cnt)], rc.at[pl.ds(landed, cnt)], other)
+            a = send(g4.at[pl.ds(w.start(1 - me.c) + off, cnt)], rc.at[pl.ds(landed, cnt)], other, "back")
             sent.append(a)
             yield
             a.wait_recv()
@@ -631,8 +661,8 @@
             right, left, far = rect((at + 1) % 4), rect((at + 3) % 4), rect((at + 2) % 4)
             if n in forward:
                 now = [
-                    send(view(g4, far, 0), slot(2, 0), me.step(axis, 1)),
-                    send(view(g4, far, 1), slot(2, 1), me.step(axis, 3)),
+                    send(view(g4, far, 0), slot(2, 0), me.step(axis, 1), "back"),
+                    send(view(g4, far, 1), slot(2, 1), me.step(axis, 3), "back"),
                 ]
                 sent += now
                 yield
@@ -647,12 +677,12 @@
                     return carry
 
                 lax.fori_loop(0, size, add_far, 0)
-                now = [send(view(g4, right), slot(0), me.step(axis, 1)), send(view(g4, left), slot(1), me.step(axis, 3))]
+                now = [send(view(g4, right), slot(0), me.step(axis, 1), "back"), send(view(g4, left), slot(1), me.step(axis, 3), "back")]
             else:
                 now = [
-                    send(view(g4, right), slot(0), me.step(axis, 1)),
-                    send(view(g4, left), slot(1), me.step(axis, 3)),
-                    send(view(g4, far), slot(2), me.step(axis, 2)),
+                    send(view(g4, right), slot(0), me.step(axis, 1), "back"),
+                    send(view(g4, left), slot(1), me.step(axis, 3), "back"),
+                    send(view(g4, far), slot(2), me.step(axis, 2), "back"),
                 ]
             sent += now
             yield
@@ -672,7 +702,7 @@
         for cp in sent:
             cp.wait_send()
 
-    back_y, back_z, back_x = reduce(FIRST, "y", (0,)), reduce(FIRST, "z", (0,)), reduce(FIRST, "x", (0,))
+    back_y, back_z, back_x = reduce(FIRST, "y"), reduce(FIRST, "z"), reduce(FIRST, "x")
 
     x2, mc = R.nrm2[...].reshape(2 * S, D), R.mcot[...].reshape(2 * S, D)
     for j in reversed(range(4)):
@@ -869,7 +899,7 @@
     R.stat[...] = jnp.where(
         r8 == 0, rate_sum, jnp.where(r8 == 1, count, jnp.where(r8 == 2, rate_max, jnp.where(r8 == 3, bias_row, 0.0)))
     )
-    stats = [send(R.stat, R.sa.at[me.s], me.peer(*p)[0]) for p in PEERS]
+    stats = send_all([(R.stat, R.sa.at[me.s], dev) for dev, _ in peers], R.sa.at[pl.ds(0, 15)])
     R.sa[pl.ds(me.s, 1)] = R.stat[...][None]
     for i in range(4):
         rows = pl.ds(32 * i, 32)
@@ -889,10 +919,9 @@
             total, peak = total + buf[s], jnp.maximum(peak, buf[s])
         return jnp.where(r8 == 2, peak, total)
 
-    for cp in stats:
-        cp.wait_recv()
+    stats.wait_recv()
     R.sb[pl.ds(me.zx, 1)] = combine(R.sa, 16)[None]
-    stats2 = [send(R.sb.at[me.zx], R.sb.at[me.zx], me.far(*p)) for p in FARS]
+    stats2 = send_all([(R.sb.at[me.zx], R.sb.at[me.zx], me.far(*p)) for p in FARS], R.sb.at[pl.ds(0, 7)])
     finish(mid_x, mid_z, back_y, last_x, last_z, back_z, back_x)
 
     i = 0
@@ -904,21 +933,16 @@
             i += 1
     for s in range(16):
         pk[s] = pkf[s].astype(BF16)
-    last = []
-    for p in PEERS:
-        dev, slot = me.peer(*p)
-        last.append(send(pk.at[slot], rv2.at[me.s], dev))
+    last = send_all([(pk.at[slot], rv2.at[me.s], dev) for dev, slot in peers], rv2.at[pl.ds(0, 15)])
     rv2[pl.ds(me.s, 1)] = pk[pl.ds(me.s, 1)]
-    for cp in stats2:
-        cp.wait_recv()
+    stats2.wait_recv()
     R.stat_sum[...] = combine(R.sb, 8)
     stat_copy = pltpu.make_async_copy(R.stat_sum, stat_any, R.lsem.at[2])
     stat_copy.start()
-    for cp in last:
-        cp.wait_recv()
+    last.wait_recv()
     raw_copy = pltpu.make_async_copy(rv2, raw_any, R.lsem.at[3])
     raw_copy.start()
-    for cp in [mc_copy, n2_copy, t_copy, o_copy] + stats + stats2 + last:
+    for cp in (mc_copy, n2_copy, t_copy, o_copy, stats, stats2, last):
         cp.wait_send()
     for cp in (out_copy, gtok_copy, stat_copy, raw_copy):
         cp.wait()

time: 129 us -> 115 us (0.89)
  Pallas kernels: 128 us -> 114 us
    pallas_call x1, Pallas kernels: 126 us -> 112 us  [step(): pl.pallas_call(step_kernel, out_shape=(sd((S, D), BF16), sd((S, D), BF16)...]
where the time goes in v2:
time: 115 us
  Pallas kernels  114 us (99%)
    pallas_call x1, Pallas kernels, step(): pl.pallas_call(step_kernel, out_shape=(sd((S, D), BF16), sd((S, D), BF16)...  112 us

profile of v2, /device:TPU:1, one launch (start us, length us, event | category | flops | bytes accessed | tf_op | source)
XLA Modules:
  0.0 114.7 jit_solution(16079644818550320084)
XLA Ops:
  0.7 111.8 %step.1 = (bf16[128,768]{1,0:T(8,128)(2,1)}, bf16[128,768]{1,0:T(8,128)(2,1)}, bf16[16,96,128]{2,1,0:T(8,128)(2,1)}, f32[8,128]{1,0:T(8,128)}) custom-call(s32[1,4]{1,0:T(1,128)} %refs_0_.1, bf16[1,6]{1,0:T(2,128)(2,1)} %bitcast.18, bf16[1,6]{1,0:T(2,128)(2,1)} %bitcast.19, bf16[1,6]{1,0:T(2,128)(2,1)} %bitcast.20, bf16[1,6]{1,0:T(2,128)(2,1)} %bitcast.21, ...), custom_call_target="tpu_custom_call" | custom-call | tf_op jit(solution)/shard_map/step/pallas_call | solution.py:954
  112.4 2.1 %finish.1 = (bf16[128,768]{1,0:T(8,128)(2,1)}, bf16[128,768]{1,0:T(8,128)(2,1)}, f32[1,6]{1,0:T(1,128)}, f32[6,768]{1,0:T(8,128)}, f32[6,768]{1,0:T(8,128)}, /*i...) custom-call(bf16[16,96,128]{2,1,0:T(8,128)(2,1)} %get-tuple-element., ...), custom_call_target="tpu_custom_call" | custom-call | tf_op jit(solution)/shard_map/finish/pallas_call | solution.py:1012

commit v3 on v2

--- a/solution.py
+++ b/solution.py
@@ -82,6 +82,13 @@
 TILES = 52
 PER = max(sum(w.per for w in ws) for ws in (OUT_WAVES, BACK_WAVES))
 PROWS = (PER * 6 + 15) // 16 * 16
+EARLY, LATE = BACK_WAVES[1:], BACK_WAVES[:1]
+
+
+def rows_of(waves):
+    return (sum(w.per for w in waves) * 6 + 15) // 16 * 16
+
+
 TQ, TK, TS, TV = 0, 6, 12, 16
 PADS = (25, 26, 27)
 A_Q, A_K, A_V, A_O, A_G, A_U, A_D, A_S = range(8)
@@ -238,7 +245,7 @@
 
 def copies_of(w, color, back):
     fwd = steps_forward(w, color, back)
-    return sum(4 if n in fwd else 3 for n in range(len(w.chain(color, Zero)))) + (0 if w.split else 1)
+    return sum(2 if n in fwd else 1 for n in range(len(w.chain(color, Zero)))) + (0 if w.split else 1 if back else 4)
 
 
 OUT_COPIES = sum(copies_of(w, k, False) for w in OUT_WAVES for k in w.colors())
@@ -269,7 +276,8 @@
     wo=b16(6, 768), wg=b16(6, FF), wu=b16(6, FF), wd=b16(6, FF), init=b16(6, HEAD), rate=b16(6, HEADS), small=f32(6, 128),
     w4=b16(TILES, 4, 2, 96, 128), g4=b16(TILES, 4, 2, 96, 128), rc=b16(LAST.half + MID.half, 4, 2, 96, 128),
     land=b16(BACK_SLOTS, 96, 128), pk=b16(16, PROWS, 128), pkf=f32(16, PROWS, 128), rv=b16(16, PROWS, 128),
-    rv2=b16(16, PROWS, 128), stf=f32(96, 128), sa=f32(16, 8, 128), sb=f32(8, 8, 128), stat=f32(8, 128), stat_sum=f32(8, 128),
+    pk_a=b16(16, rows_of(EARLY), 128), rv_a=b16(16, rows_of(EARLY), 128), pk_b=b16(16, rows_of(LATE), 128),
+    rv_b=b16(16, rows_of(LATE), 128), stf=f32(96, 128), sa=f32(16, 8, 128), sb=f32(8, 8, 128), stat=f32(8, 128), stat_sum=f32(8, 128),
     nrm=b16(S, D), q=f32(S, D), k=f32(S, D), v=f32(S, D), zc=f32(S, D), zq=f32(S, D), u=f32(S, D), gh=b16(S, D), gl=b16(S, D),
     s1=f32(S, D), c1=f32(S, D), e1=f32(S, D), y1=f32(S, D), n1=f32(S, D), n2=f32(S, D), s2=f32(S, D),
     mix=f32(S, D), hid=f32(S, D), post=b16(S, D), dzb=b16(S, D), dzc=b16(S, D), dgr=f32(S, D), dzf=f32(S, D),
@@ -291,8 +299,8 @@
 def step_kernel(*refs):
     lens_ref = refs[0]
     hbm = refs[1 : 1 + len(INPUTS)]
-    out_any, gtok_any, raw_any, stat_any = refs[1 + len(INPUTS) : 5 + len(INPUTS)]
-    R = Refs(refs[5 + len(INPUTS) :])
+    out_any, gtok_any, raw_a, raw_b, stat_any = refs[1 + len(INPUTS) : 6 + len(INPUTS)]
+    R = Refs(refs[6 + len(INPUTS) :])
     w4, g4, rc, land = R.w4, R.g4, R.rc, R.land
     me = Place()
     taken = {"group": 0, "out": 8, "back": 8}
@@ -344,7 +352,7 @@
     bias_col = tt(one_hot(iota((HEADS, S), 0) + RATE0 == iota((HEADS, S), 1)), R.bias_rate[...])
 
     srcs = (R.wq, R.wk, R.wv, R.wo, R.wg, R.wu, R.wd, R.small)
-    pkf, pk, rv, rv2, stf = R.pkf, R.pk, R.rv, R.rv2, R.stf
+    pkf, pk, rv, stf = R.pkf, R.pk, R.rv, R.stf
     pkf[0] = jnp.zeros((PROWS, 128), F32)
     for h in range(2):
         for xl in range(2):
@@ -359,6 +367,15 @@
                         i += 1
                 pk[h * 8 + xl * 4 + y] = pkf[0].astype(BF16)
     pl.semaphore_wait(barrier, greeted)
+    def send_step(triples, size, kind):
+        i = taken[kind]
+        taken[kind] += 1
+        j = i + OUT_COPIES if kind == "back" else i
+        for src, dst, dev in triples:
+            copy(src, dst, dev, i, j).start()
+        whole = land.at[pl.ds(0, size)]
+        return copy(whole, whole, me.dev(), i, j)
+
     peers = [me.peer(*p) for p in PEERS]
     firsts = send_all([(pk.at[slot], rv.at[me.s], dev) for dev, slot in peers], rv.at[pl.ds(0, 15)])
     rv[pl.ds(me.s, 1)] = pk[pl.ds(me.s, 1)]
@@ -386,32 +403,41 @@
 
     def gather(w, color):
         forward = steps_forward(w, color, False)
-        sent = []
-        for n, (axis, rect) in enumerate(w.chain(color, me)):
+        sent, crossed = [], []
+        chain = w.chain(color, me)
+        for n, (axis, rect) in enumerate(chain):
             at = me.coord(axis)
-            mine, lo, hi = rect(at), rect((at + 3) % 4), rect((at + 1) % 4)
-            now = [send(view(w4, mine), view(w4, mine), me.step(axis, d), "out") for d in ((1, 3) if n in forward else (1, 3, 2))]
-            sent += now
+            mine, lo, hi, far = (rect((at + d) % 4) for d in (0, 3, 1, 2))
+            last = n == len(chain) - 1 and not w.split
+
+            def cross(*rects, last=last):
+                if last:
+                    crossed.extend(send(view(w4, r), view(w4, r), other, "out") for r in rects)
+
+            size = blocks(mine)[0]
+            where = (1, 3) if n in forward else (1, 3, 2)
+            now = send_step([(view(w4, mine), view(w4, mine), me.step(axis, d)) for d in where], len(where) * size, "out")
+            sent.append(now)
+            cross(mine)
             yield
-            for cp in now:
+            now.wait_recv()
+            if n in forward:
+                now = send_step(
+                    [(view(w4, lo, 0), view(w4, lo, 0), me.step(axis, 1)), (view(w4, hi, 1), view(w4, hi, 1), me.step(axis, 3))],
+                    size, "out",
+                )
+                sent.append(now)
+                cross(lo, hi)
+                yield
+                now.wait_recv()
+                cross(far)
+            else:
+                cross(lo, hi, far)
+        if crossed:
+            yield
+            for cp in crossed:
                 cp.wait_recv()
-            if n in forward:
-                now = [
-                    send(view(w4, lo, 0), view(w4, lo, 0), me.step(axis, 1), "out"),
-                    send(view(w4, hi, 1), view(w4, hi, 1), me.step(axis, 3), "out"),
-                ]
-                sent += now
-                yield
-                for cp in now:
-                    cp.wait_recv()
-        if not w.split:
-            off, cnt = w.span(color)
-            rect = (w.start(me.c) + off, cnt, ALL, ALL)
-            a = send(view(w4, rect), view(w4, rect), other, "out")
-            sent.append(a)
-            yield
-            a.wait_recv()
-        for cp in sent:
+        for cp in sent + crossed:
             cp.wait_send()
 
     def go(*chains):
@@ -660,14 +686,13 @@
 
             right, left, far = rect((at + 1) % 4), rect((at + 3) % 4), rect((at + 2) % 4)
             if n in forward:
-                now = [
-                    send(view(g4, far, 0), slot(2, 0), me.step(axis, 1), "back"),
-                    send(view(g4, far, 1), slot(2, 1), me.step(axis, 3), "back"),
-                ]
-                sent += now
+                now = send_step(
+                    [(view(g4, far, 0), slot(2, 0), me.step(axis, 1)), (view(g4, far, 1), slot(2, 1), me.step(axis, 3))],
+                    size, "back",
+                )
+                sent.append(now)
                 yield
-                for cp in now:
-                    cp.wait_recv()
+                now.wait_recv()
                 right_at, left_at = blocks(right)[1], blocks(left)[1]
 
                 def add_far(i, carry, base=base, size=size, right_at=right_at, left_at=left_at):
@@ -677,18 +702,14 @@
                     return carry
 
                 lax.fori_loop(0, size, add_far, 0)
-                now = [send(view(g4, right), slot(0), me.step(axis, 1), "back"), send(view(g4, left), slot(1), me.step(axis, 3), "back")]
-            else:
-                now = [
-                    send(view(g4, right), slot(0), me.step(axis, 1), "back"),
-                    send(view(g4, left), slot(1), me.step(axis, 3), "back"),
-                    send(view(g4, far), slot(2), me.step(axis, 2), "back"),
-                ]
-            sent += now
+            triples = [(view(g4, right), slot(0), me.step(axis, 1)), (view(g4, left), slot(1), me.step(axis, 3))]
+            if n not in forward:
+                triples.append((view(g4, far), slot(2), me.step(axis, 2)))
+            terms = len(triples)
+            now = send_step(triples, terms * size, "back")
+            sent.append(now)
             yield
-            for cp in now:
-                cp.wait_recv()
-            terms = len(now)
+            now.wait_recv()
 
             def add_mine(i, carry, base=base, size=size, place=place, terms=terms):
                 p = place(i)
@@ -911,7 +932,7 @@
     gtok_copy = pltpu.make_async_copy(R.gtok, gtok_any, R.lsem.at[1])
     gtok_copy.start()
 
-    go(last_x, back_z, back_x, last_z)
+    go(last_x, last_z, back_z, back_x)
 
     def combine(buf, n):
         total, peak = buf[0], buf[0]
@@ -922,29 +943,40 @@
     stats.wait_recv()
     R.sb[pl.ds(me.zx, 1)] = combine(R.sa, 16)[None]
     stats2 = send_all([(R.sb.at[me.zx], R.sb.at[me.zx], me.far(*p)) for p in FARS], R.sb.at[pl.ds(0, 7)])
-    finish(mid_x, mid_z, back_y, last_x, last_z, back_z, back_x)
-
-    i = 0
-    for w in BACK_WAVES:
-        for t in w.mine(me.c, me.xl, me.y):
-            stf[...] = g4[t, me.z, me.xh].astype(F32)
-            for s in range(16):
-                pkf[s, pl.ds(6 * i, 6), :] = stf[pl.ds(6 * s, 6), :]
-            i += 1
-    for s in range(16):
-        pk[s] = pkf[s].astype(BF16)
-    last = send_all([(pk.at[slot], rv2.at[me.s], dev) for dev, slot in peers], rv2.at[pl.ds(0, 15)])
-    rv2[pl.ds(me.s, 1)] = pk[pl.ds(me.s, 1)]
+    for _ in range(2):
+        go(last_x, last_z, mid_x, mid_z, back_y, back_z, back_x)
+    finish(mid_x, mid_z, back_y, back_z, back_x)
+
+    def owners(waves, pack, land_):
+        i = 0
+        for w in waves:
+            for t in w.mine(me.c, me.xl, me.y):
+                stf[...] = g4[t, me.z, me.xh].astype(F32)
+                for s in range(16):
+                    pkf[s, pl.ds(6 * i, 6), :] = stf[pl.ds(6 * s, 6), :]
+                i += 1
+        for s in range(16):
+            pack[s] = pkf[s, 0 : pack.shape[1], :].astype(BF16)
+        group = send_all([(pack.at[slot], land_.at[me.s], dev) for dev, slot in peers], land_.at[pl.ds(0, 15)])
+        land_[pl.ds(me.s, 1)] = pack[pl.ds(me.s, 1)]
+        return group
+
+    early = owners(EARLY, R.pk_a, R.rv_a)
     stats2.wait_recv()
     R.stat_sum[...] = combine(R.sb, 8)
     stat_copy = pltpu.make_async_copy(R.stat_sum, stat_any, R.lsem.at[2])
     stat_copy.start()
-    last.wait_recv()
-    raw_copy = pltpu.make_async_copy(rv2, raw_any, R.lsem.at[3])
-    raw_copy.start()
-    for cp in (mc_copy, n2_copy, t_copy, o_copy, stats, stats2, last):
+    finish(last_x, last_z)
+    late = owners(LATE, R.pk_b, R.rv_b)
+    early.wait_recv()
+    raw_a_copy = pltpu.make_async_copy(R.rv_a, raw_a, R.lsem.at[3])
+    raw_a_copy.start()
+    late.wait_recv()
+    raw_b_copy = pltpu.make_async_copy(R.rv_b, raw_b, R.lsem.at[4])
+    raw_b_copy.start()
+    for cp in (mc_copy, n2_copy, t_copy, o_copy, stats, stats2, early, late):
         cp.wait_send()
-    for cp in (out_copy, gtok_copy, stat_copy, raw_copy):
+    for cp in (out_copy, gtok_copy, stat_copy, raw_a_copy, raw_b_copy):
         cp.wait()
 
 
@@ -953,28 +985,36 @@
     sd = jax.ShapeDtypeStruct
     return pl.pallas_call(
         step_kernel,
-        out_shape=(sd((S, D), BF16), sd((S, D), BF16), sd((16, PROWS, 128), BF16), sd((8, 128), F32)),
+        out_shape=(
+            sd((S, D), BF16), sd((S, D), BF16), sd((16, rows_of(EARLY), 128), BF16), sd((16, rows_of(LATE), 128), BF16),
+            sd((8, 128), F32),
+        ),
         in_specs=[pl.BlockSpec(memory_space=pltpu.SMEM)] + [anym] * len(INPUTS),
-        out_specs=(anym,) * 4,
+        out_specs=(anym,) * 5,
         scratch_shapes=list(SCRATCH.values()),
         compiler_params=pltpu.CompilerParams(collective_id=0, has_side_effects=True, vmem_limit_bytes=60 * 2**20),
         name="step",
     )(lens, *arrays)
 
 
-def finish_kernel(raw, stat, out_in, gtok_in, *outs):
+def finish_kernel(raw_a, raw_b, stat, out_in, gtok_in, *outs):
     (out, gtok, g_norm, gq, gk, gv, g_rate, g_brate, g_init, g_ib, g_ig, g_ibias, g_pg, g_pb, go, g_mg, gg, gu, gd,
-     r_mean, r_max, pkf) = outs
+     r_mean, r_max, early, late) = outs
     out[...] = out_in[...]
     gtok[...] = gtok_in[...]
     mats = (gq, gk, gv, go, gg, gu, gd)
     for s in range(16):
-        pkf[s] = raw[s].astype(F32)
+        early[s] = raw_a[s].astype(F32)
+        late[s] = raw_b[s].astype(F32)
     for h in range(2):
         for xl in range(2):
-            i = 0
+            counts = [0, 0]
             for w in BACK_WAVES:
+                kind = int(w in LATE)
+                pkf = (early, late)[kind]
                 for n in range(w.per):
+                    i = counts[kind]
+                    counts[kind] += 1
                     for y in range(4 if n >= w.nx + w.nz else 1):
                         where = tile_source(w, h, w.mine(h, xl, y)[n])
                         if where is None:
@@ -993,14 +1033,13 @@
                             vt = val.T
                             for n_, ref in enumerate((g_norm, g_ib, g_ig, g_ibias, g_pg, g_pb, g_mg)):
                                 ref[...] = vt[VEC0 + n_ : VEC0 + n_ + 1, :]
-                    i += 1
     st = stat[...]
     g_brate[...] = st[3:4, RATE0 : RATE0 + HEADS]
     r_mean[...] = st[0:1, 0:1] / st[1:2, 0:1]
     r_max[...] = st[2:3, 0:1]
 
 
-def finish_call(raw, stat, out, gtok):
+def finish_call(raw_a, raw_b, stat, out, gtok):
     vm = pl.BlockSpec(memory_space=pltpu.VMEM)
     sd = jax.ShapeDtypeStruct
     row = sd((1, 6), F32)
@@ -1010,9 +1049,9 @@
         sd((6, HEAD), F32), row, row, row, row, row, m768, row, m2048, m2048, m2048, sd((1, 1), F32), sd((1, 1), F32),
     )
     return pl.pallas_call(
-        finish_kernel, out_shape=shapes, in_specs=[vm] * 4, out_specs=(vm,) * 21,
-        scratch_shapes=[pltpu.VMEM((16, PROWS, 128), F32)], name="finish",
-    )(raw, stat, out, gtok)
+        finish_kernel, out_shape=shapes, in_specs=[vm] * 5, out_specs=(vm,) * 21,
+        scratch_shapes=[f32(16, rows_of(EARLY), 128), f32(16, rows_of(LATE), 128)], name="finish",
+    )(raw_a, raw_b, stat, out, gtok)
 
 
 def per_device(
@@ -1021,11 +1060,11 @@
     weight_down,
 ):
     rows = (norm_gain, init_bias, inner_gain, inner_bias, post_gain, post_bias, mlp_gain)
-    out, gtok, raw, stat = step(
+    out, gtok, raw_a, raw_b, stat = step(
         seq_lengths, *[r.reshape(1, -1) for r in rows + (bias_rate,)], tokens, cotangent, weight_query, weight_key, weight_value, weight_out, weight_gate, weight_up,
         weight_down, init_weight, weight_rate,
     )
-    res = list(finish_call(raw, stat, out, gtok))
+    res = list(finish_call(raw_a, raw_b, stat, out, gtok))
     for i in (2, 9, 10, 11, 12, 13, 15):
         res[i] = res[i].reshape(6)
     res[7] = res[7].reshape(HEADS)

time: 115 us -> 116 us (level)
  no operation moved by 1% of the time
where the time goes in v3:
time: 116 us; the launch traced here: 115 us
  Pallas kernels  115 us (99%)
    pallas_call x1, Pallas kernels, step(): pl.pallas_call(step_kernel, out_shape=(sd((S, D), BF16), sd((S, D), BF16)...  112 us

profile of v3, /device:TPU:1, one launch (start us, length us, event | category | flops | bytes accessed | tf_op | source)
XLA Modules:
  0.0 115.4 jit_solution(17970610731709714995)
XLA Ops:
  0.7 112.4 %step.1 = (bf16[128,768]{1,0:T(8,128)(2,1)}, bf16[128,768]{1,0:T(8,128)(2,1)}, bf16[16,80,128]{2,1,0:T(8,128)(2,1)}, bf16[16,32,128]{2,1,0:T(8,128)(2,1)}, f32[8,128]{1,0:T(8,128)}) custom-call(s32[1,4]{1,0:T(1,128)} %refs_0_.1, bf16[1,6]{1,0:T(2,128)(2,1)} %bitcast.18, bf16[1,6]{1,0:T(2,128)(2,1)} %bitcast.19, bf16[1,6]{1,0:T(2,128)(2,1)} %bitcast.20, ...), custom_call_target="tpu_custom_call" | custom-call | tf_op jit(solution)/shard_map/step/pallas_call | solution.py:986
  113.1 2.2 %finish.1 = (bf16[128,768]{1,0:T(8,128)(2,1)}, bf16[128,768]{1,0:T(8,128)(2,1)}, f32[1,6]{1,0:T(1,128)}, f32[6,768]{1,0:T(8,128)}, f32[6,768]{1,0:T(8,128)}, /*i...) custom-call(bf16[16,80,128]{2,1,0:T(8,128)(2,1)} %get-tuple-element., ...), custom_call_target="tpu_custom_call" | custom-call | tf_op jit(solution)/shard_map/finish/pallas_call | solution.py:1051
